TPU v7x, 256 devices: a whole 4x4x8 slice. The times are simulated.
256 devices in a mesh: rep: 2 (over x_hi), ep: 128 (over y, z, x_lo, core).
Axes of the slice: x: 4 (x_hi: 2, x_lo: 2; x = x_hi * 2 + x_lo), y: 4, z: 8, core: 2. Of those that a mesh axis runs over, the one named last changes fastest.
Arguments:
- tokens: bfloat16 [2, 8192, 3584], P(None, ('rep', 'ep')), may hold values from -6 to 6
- routing: int32 [2, 8192, 8], P(None, ('rep', 'ep')), may hold values from 0 to 63, all different within a row; in each aligned block of 32 rows (0 to 31, 32 to 63, ..., all dimensions but the last counted through in order) at most 8 rows name the same one
- route_gate: float32 [2, 8192, 8], P(None, ('rep', 'ep')), may hold values from 0.05 to 0.5
- place_old: int32 [2, 64], replicated, may hold values from 0 to 63, as said below
- place_new: int32 [2, 64], replicated, may hold values from 0 to 63, as said below
- gate_proj: bfloat16 [2, 128, 3584, 512], P('rep', 'ep'), may hold values from -0.09375 to 0.09375
- up_proj: bfloat16 [2, 128, 3584, 512], P('rep', 'ep'), may hold values from -0.09375 to 0.09375
- down_proj: bfloat16 [2, 128, 512, 3584], P('rep', 'ep'), may hold values from -0.1875 to 0.1875
Outputs:
- combined: bfloat16 [2, 8192, 3584], P(None, ('rep', 'ep'))
Inputs may be any that keep to these rules, and one draw needn't show every extreme that they name: `routing`: in the rows of one device of one batch (aligned blocks of 32 rows) no expert is named more than 8 times, a bound that some block reaches; a row names distinct experts. `place_old`: each row is a permutation of the experts. Each row is a permutation of the experts; at exactly 16 positions, the same in both rows, place_new[r, e] = place_old[1 - r, e] differs from place_old[r, e]; elsewhere it equals place_old.
All inputs are finite; a program needn't handle non-finite values.
Results may differ from a plain program's by a relative error of at most 0.0058.
Values may be sent and summed in bfloat16 or wider, within the bound.
A program may use at most 128 MiB of HBM per device.

v0:
```python
import jax
import jax.numpy as jnp
from jax import lax
from jax.sharding import PartitionSpec as P


def from_partner(block, axis, distance):
    count = lax.axis_size(axis)
    route = []
    for low in range(count):
        high = low | 1 << distance
        if high != low and high < count:
            route += [(low, high), (high, low)]
    return lax.ppermute(block, axis, route)


def expert_rows(row_block, gate_mat, up_mat, down_mat):
    gate_part = jnp.dot(row_block, gate_mat, preferred_element_type=jnp.float32)
    up_part = jnp.dot(row_block, up_mat, preferred_element_type=jnp.float32)
    hidden = (jax.nn.silu(gate_part) * up_part).astype(jnp.bfloat16)
    return jnp.dot(hidden, down_mat, preferred_element_type=jnp.float32).astype(jnp.bfloat16)


def body(tokens, routing, route_gate, place_old, place_new, gate_proj, up_proj, down_proj):
    ep_count = lax.axis_size("ep")
    positions = ep_count // 2
    here_rep = lax.axis_index("rep")
    here_pos = lax.axis_index("ep") // 2
    batch_count, tok_rows, model_width = tokens.shape
    top_count = routing.shape[2]
    capacity = min(tok_rows, (2 * tok_rows * top_count + positions - 1) // positions)
    own_weights = (gate_proj[0, 0], up_proj[0, 0], down_proj[0, 0])
    old_layout = lax.dynamic_index_in_dim(place_old, here_rep, 0, keepdims=False)
    new_layout = lax.dynamic_index_in_dim(place_new, here_rep, 0, keepdims=False)
    is_moved = lax.dynamic_index_in_dim(
        new_layout, here_pos, 0, keepdims=False
    ) != lax.dynamic_index_in_dim(old_layout, here_pos, 0, keepdims=False)
    weights_now = own_weights
    partner = from_partner((gate_proj[0, 0], up_proj[0, 0], down_proj[0, 0]), "rep", 0)
    weights_now = tuple(
        (jnp.where(is_moved, theirs, mine) for theirs, mine in zip(partner, own_weights))
    )
    lane_index = jnp.arange(positions, dtype=jnp.int32)
    outputs = []
    for batch_at in range(batch_count):
        layout = old_layout if batch_at == 0 else new_layout
        chosen = routing[batch_at].reshape(tok_rows * top_count)
        matches = chosen[:, None] == layout[None, :]
        flat_hit = matches.astype(jnp.int32)
        target = jnp.sum(flat_hit * lane_index[None, :], axis=1)
        earlier = jnp.cumsum(flat_hit, axis=0) - flat_hit
        order_in = jnp.sum(earlier * flat_hit, axis=1)
        slot_index = target * capacity + order_in
        token_of = jnp.arange(tok_rows * top_count, dtype=jnp.int32) // top_count
        packed = (
            jnp.zeros((positions * capacity, model_width), jnp.bfloat16)
            .at[slot_index]
            .set(tokens[batch_at][token_of])
        )
        packed = packed.reshape(positions, 1, capacity, model_width)
        outgoing = jnp.broadcast_to(packed, (positions, 2, capacity, model_width)).reshape(
            ep_count, capacity, model_width
        )

        def serve_rows(received, batch_at=batch_at):
            shape_in = received.shape
            if batch_at == 0:
                produced = expert_rows(received.reshape(-1, model_width), *own_weights)
            else:
                produced = expert_rows(received.reshape(-1, model_width), *weights_now)
            produced = produced.reshape(shape_in)
            return lax.all_to_all(produced, "ep", split_axis=0, concat_axis=0, tiled=True)

        result = serve_rows(lax.all_to_all(outgoing, "ep", split_axis=0, concat_axis=0, tiled=True))
        halves = result.reshape(positions, 2, capacity, model_width)
        first = halves[:, 0].reshape(positions * capacity, model_width)[slot_index]
        second = halves[:, 1].reshape(positions * capacity, model_width)[slot_index]
        picked = first.astype(jnp.float32) + second.astype(jnp.float32)
        picked = picked.reshape(tok_rows, top_count, model_width)
        combined = jnp.sum(route_gate[batch_at][:, :, None] * picked, axis=1)
        outputs.append(combined.astype(jnp.bfloat16))
    return jnp.stack(outputs)


def solution(mesh):
    return jax.shard_map(
        body,
        mesh=mesh,
        in_specs=(
            P(None, ("rep", "ep"), None),
            P(None, ("rep", "ep"), None),
            P(None, ("rep", "ep"), None),
            P(),
            P(),
            P("rep", "ep", None, None),
            P("rep", "ep", None, None),
            P("rep", "ep", None, None),
        ),
        out_specs=P(None, ("rep", "ep"), None),
        check_vma=False,
    )
```

profile of v0, /device:TPU:4, one launch (start us, length us, event | category | flops | bytes accessed | tf_op | source)
XLA Modules:
  0.0 912.2 jit_solution(2231616970547791410)
XLA Ops:
  0.0 0.7 fusion.44
  0.7 0.1 copy.16
  0.8 0.1 eq.59
  0.9 0.1 eq.54
  1.0 0.7 dynamic-slice_bitcast_fusion
  1.7 0.1 compare_convert_fusion.3
  1.8 0.6 reduce-window.14
  2.4 0.2 slice_reduce_fusion.1
  2.6 0.1 fusion.29
  2.7 1.1 slice_bitcast_fusion.5
  3.8 10.8 %scatter_custom_fusion = bf16[512,3584]{1,0:T(8,128)(2,1)} fusion(s32[256]{0:T(256)S(1)} %bitcast.122, bf16[32,3584]{1,0:T(8,128)(2,1)S(1)} %get-tuple-element.13, s32[1024]{0:T(1024)S(1)} %pad_clamp_fusion.2, bf16[]{:T(256)} %constant.84.clone.1), kind=kCustom, calls=%fused_computation.38 | custom fusion | bytes 3670018 | tf_op jit(solution)/shard_map/scatter | solution.py:58
  14.7 5.6 broadcast_in_dim.9
  20.3 14.4 %all-to-all-start = ((bf16[128,8,3584]{2,1,0:T(8,128)(2,1)}), bf16[128,8,3584]{2,1,0:T(8,128)(2,1)}, u32[]{:S(2)}, u32[]{:S(2)}) async-start(bf16[128,8,3584]{2,1,0:T(8,128)(2,1)} %bitcast.116), calls=%async_computation | async-start | bytes 14680064 | tf_op jit(solution)/shard_map/all_to_all | solution.py:74
  34.8 0.1 copy.22
  34.8 0.1 eq.68
  34.9 0.1 eq.63
  35.0 0.1 compare_convert_fusion.2
  35.1 0.6 reduce-window.16
  35.7 0.2 slice_reduce_fusion
  35.9 0.1 fusion.32
  36.1 22.2 %scatter_custom_fusion.1 = bf16[512,3584]{1,0:T(8,128)(2,1)} fusion(s32[256]{0:T(256)S(1)} %bitcast.124, bf16[32,3584]{1,0:T(8,128)(2,1)S(1)} %get-tuple-element.14, s32[1024]{0:T(1024)S(1)} %pad_clamp_fusion.2, bf16[]{:T(256)} %constant.84.clone.1), kind=kCustom, calls=%fused_computation.36 | custom fusion | bytes 3670018 | tf_op jit(solution)/shard_map/scatter | solution.py:58
  58.3 140.6 %all-to-all-done = bf16[128,8,3584]{2,1,0:T(8,128)(2,1)} async-done(((bf16[128,8,3584]{2,1,0:T(8,128)(2,1)}), bf16[128,8,3584]{2,1,0:T(8,128)(2,1)}, u32[]{:S(2)}, u32[]{:S(2)}) %all-to-all-start) | async-done | bytes 7340064 | tf_op jit(solution)/shard_map/all_to_all | solution.py:74
  199.0 5.6 broadcast_in_dim.11
  204.5 7.4 all-to-all-start.2
  211.9 9.4 %fusion.4 = f32[1024,512]{1,0:T(8,128)} fusion(bf16[128,8,3584]{2,1,0:T(8,128)(2,1)} %all-to-all-done, bf16[1,1,3584,512]{3,2,1,0:T(8,128)(2,1)} %param.14), kind=kOutput, calls=%fused_computation.14 | convolution fusion | flops 3758096384 | bytes 13107200 | tf_op jit(solution)/shard_map/dot_general | solution.py:19
  221.4 14.7 %fusion.8 = bf16[128,8,3584]{2,1,0:T(8,128)(2,1)} fusion(f32[1024,512]{1,0:T(8,128)} %fusion.4, bf16[128,8,3584]{2,1,0:T(8,128)(2,1)} %all-to-all-done, bf16[1,1,512,3584]{3,2,1,0:T(8,128)(2,1)} %param.15, bf16[1,1,3584,512]{3,2,1,0:T(8,128)(2,1)} %param.13), kind=kOutput, calls=%fused_computation.18 | convolution fusion | flops 7523008512 | bytes 24117248 | tf_op jit(solution)/shard_map/dot_general | solution.py:21
  236.1 0.0 copy-start.3
  236.1 0.0 copy-start.4
  236.1 140.1 %all-to-all-done.2 = bf16[128,8,3584]{2,1,0:T(8,128)(2,1)} async-done(((bf16[128,8,3584]{2,1,0:T(8,128)(2,1)}), bf16[128,8,3584]{2,1,0:T(8,128)(2,1)}, u32[]{:S(2)}, u32[]{:S(2)}) %all-to-all-start.2) | async-done | bytes 7340064 | tf_op jit(solution)/shard_map/all_to_all | solution.py:74
  376.1 7.4 all-to-all-start.1
  383.6 0.9 collective-permute-start.1
  384.4 2.7 collective-permute-start
  387.2 0.8 collective-permute-start.2
  388.0 0.0 copy-done.3
  388.0 0.6 dynamic_slice.16
  388.6 0.0 copy-done.4
  388.6 0.6 dynamic_slice.17
  390.4 151.4 %collective-permute-done.1 = bf16[3584,512]{1,0:T(8,128)(2,1)} collective-permute-done((bf16[3584,512]{1,0:T(8,128)(2,1)}, bf16[3584,512]{1,0:T(8,128)(2,1)}, u32[]{:S(2)}, u32[]{:S(2)}) %collective-permute-start.1) | collective-permute-done | bytes 3670048 | tf_op jit(solution)/shard_map/ppermute | solution.py:14
  541.8 0.0 copy-start.5
  541.8 8.7 fusion
  550.5 0.0 copy-start.6
  550.5 70.5 %collective-permute-done = bf16[3584,512]{1,0:T(8,128)(2,1)} collective-permute-done((bf16[3584,512]{1,0:T(8,128)(2,1)}, bf16[3584,512]{1,0:T(8,128)(2,1)}, u32[]{:S(2)}, u32[]{:S(2)}) %collective-permute-start) | collective-permute-done | bytes 3670048 | tf_op jit(solution)/shard_map/ppermute | solution.py:14
  621.0 0.0 copy-done.5
  621.0 7.5 fusion.2
  628.5 70.1 %collective-permute-done.2 = bf16[512,3584]{1,0:T(8,128)(2,1)} collective-permute-done((bf16[512,3584]{1,0:T(8,128)(2,1)}, bf16[512,3584]{1,0:T(8,128)(2,1)}, u32[]{:S(2)}, u32[]{:S(2)}) %collective-permute-start.2) | collective-permute-done | bytes 3670048 | tf_op jit(solution)/shard_map/ppermute | solution.py:14
  698.6 0.0 copy-done.6
  698.6 8.4 fusion.9
  707.1 0.0 all-to-all-done.1
  707.1 13.6 %all-to-all-start.3 = ((bf16[128,8,3584]{2,1,0:T(8,128)(2,1)}), bf16[128,8,3584]{2,1,0:T(8,128)(2,1)}, u32[]{:S(2)}, u32[]{:S(2)}) async-start(bf16[128,8,3584]{2,1,0:T(8,128)(2,1)} %fusion.9), calls=%async_computation.3 | async-start | bytes 14680064 | tf_op jit(solution)/shard_map/all_to_all | solution.py:72
  720.7 0.0 copy-done.2
  720.7 0.1 copy.15
  720.8 0.1 copy.21
  720.9 6.6 slice_bitcast_fusion.3
  727.5 6.0 gather_fusion
  733.5 7.3 gather_fusion.1
  740.9 143.8 %all-to-all-done.3 = bf16[128,8,3584]{2,1,0:T(8,128)(2,1)} async-done(((bf16[128,8,3584]{2,1,0:T(8,128)(2,1)}), bf16[128,8,3584]{2,1,0:T(8,128)(2,1)}, u32[]{:S(2)}, u32[]{:S(2)}) %all-to-all-start.3) | async-done | bytes 7340064 | tf_op jit(solution)/shard_map/all_to_all | solution.py:72
  884.7 6.5 slice_bitcast_fusion.1
  891.2 7.6 gather_fusion.2
  898.8 7.3 gather_fusion.3
  906.1 3.2 fusion.11
  909.3 0.0 copy-done
  909.3 0.0 copy-done.1
  909.3 1.6 fusion.10
  910.9 0.8 pad_maximum_fusion
  (16 shorter events, 0.1 us)
Async XLA Ops:
  20.3 178.6 %all-to-all-start = ((bf16[128,8,3584]{2,1,0:T(8,128)(2,1)}), bf16[128,8,3584]{2,1,0:T(8,128)(2,1)}, u32[]{:S(2)}, u32[]{:S(2)}) async-start(bf16[128,8,3584]{2,1,0:T(8,128)(2,1)} %bitcast.116), calls=%async_computation | async-start | bytes 14680064 | tf_op jit(solution)/shard_map/all_to_all | solution.py:74
  204.5 171.6 %all-to-all-start.2 = ((bf16[128,8,3584]{2,1,0:T(8,128)(2,1)}), bf16[128,8,3584]{2,1,0:T(8,128)(2,1)}, u32[]{:S(2)}, u32[]{:S(2)}) async-start(bf16[128,8,3584]{2,1,0:T(8,128)(2,1)} %bitcast.117), calls=%async_computation.2 | async-start | bytes 14680064 | tf_op jit(solution)/shard_map/all_to_all | solution.py:74
  236.1 151.9 %copy-start.3 = (s32[2,64]{1,0:T(2,128)S(1)}, s32[2,64]{1,0:T(2,128)}, u32[]{:S(2)}) copy-start(s32[2,64]{1,0:T(2,128)} %param.12) | copy-start | bytes 1540
  236.1 152.5 %copy-start.4 = (s32[2,64]{1,0:T(2,128)S(1)}, s32[2,64]{1,0:T(2,128)}, u32[]{:S(2)}) copy-start(s32[2,64]{1,0:T(2,128)} %param.11) | copy-start | bytes 1540
  376.1 330.9 %all-to-all-start.1 = ((bf16[128,8,3584]{2,1,0:T(8,128)(2,1)}), bf16[128,8,3584]{2,1,0:T(8,128)(2,1)}, u32[]{:S(2)}, u32[]{:S(2)}) async-start(bf16[128,8,3584]{2,1,0:T(8,128)(2,1)} %fusion.8), calls=%async_computation.1 | async-start | bytes 14680064 | tf_op jit(solution)/shard_map/all_to_all | solution.py:72
  383.6 158.2 %collective-permute-start.1 = (bf16[3584,512]{1,0:T(8,128)(2,1)}, bf16[3584,512]{1,0:T(8,128)(2,1)}, u32[]{:S(2)}, u32[]{:S(2)}) collective-permute-start(bf16[3584,512]{1,0:T(8,128)(2,1)} %bitcast.129), channel_id=1, source_target_pairs={{0,128},{128,0},{1,129},{129,1},{2,130},{130,2},{3,131},{131,3},{4... | collective-permute-start | bytes 11010056 | tf_op jit(solution)/shard_map/ppermute | solution.py:14
  384.4 236.6 %collective-permute-start = (bf16[3584,512]{1,0:T(8,128)(2,1)}, bf16[3584,512]{1,0:T(8,128)(2,1)}, u32[]{:S(2)}, u32[]{:S(2)}) collective-permute-start(bf16[3584,512]{1,0:T(8,128)(2,1)} %bitcast.130), channel_id=1, source_target_pairs={{0,128},{128,0},{1,129},{129,1},{2,130},{130,2},{3,131},{131,3},{4... | collective-permute-start | bytes 11010056 | tf_op jit(solution)/shard_map/ppermute | solution.py:14
  387.2 311.5 %collective-permute-start.2 = (bf16[512,3584]{1,0:T(8,128)(2,1)}, bf16[512,3584]{1,0:T(8,128)(2,1)}, u32[]{:S(2)}, u32[]{:S(2)}) collective-permute-start(bf16[512,3584]{1,0:T(8,128)(2,1)} %bitcast.131), channel_id=1, source_target_pairs={{0,128},{128,0},{1,129},{129,1},{2,130},{130,2},{3,131},{131,3},{4... | collective-permute-start | bytes 11010056 | tf_op jit(solution)/shard_map/ppermute | solution.py:14
  541.8 79.2 %copy-start.5 = (bf16[1,1,3584,512]{3,2,1,0:T(8,128)(2,1)S(1)}, bf16[1,1,3584,512]{3,2,1,0:T(8,128)(2,1)}, u32[]{:S(2)}) copy-start(bf16[1,1,3584,512]{3,2,1,0:T(8,128)(2,1)} %param.13) | copy-start | bytes 11010052
  550.5 148.1 %copy-start.6 = (bf16[1,1,512,3584]{3,2,1,0:T(8,128)(2,1)S(1)}, bf16[1,1,512,3584]{3,2,1,0:T(8,128)(2,1)}, u32[]{:S(2)}) copy-start(bf16[1,1,512,3584]{3,2,1,0:T(8,128)(2,1)} %param.15) | copy-start | bytes 11010052
  707.1 13.6 %copy-start.2 = (f32[2,32,8]{1,2,0:T(8,128)S(1)}, f32[2,32,8]{1,2,0:T(8,128)}, u32[]{:S(2)}) copy-start(f32[2,32,8]{1,2,0:T(8,128)} %param.10) | copy-start | bytes 6148
  707.1 177.6 %all-to-all-start.3 = ((bf16[128,8,3584]{2,1,0:T(8,128)(2,1)}), bf16[128,8,3584]{2,1,0:T(8,128)(2,1)}, u32[]{:S(2)}, u32[]{:S(2)}) async-start(bf16[128,8,3584]{2,1,0:T(8,128)(2,1)} %fusion.9), calls=%async_computation.3 | async-start | bytes 14680064 | tf_op jit(solution)/shard_map/all_to_all | solution.py:72
  906.1 3.2 copy-start
  906.1 3.2 copy-start.1
where the time goes:
time: 922 us; the launch traced here: 912 us
  waiting for transfers between devices  717 us (78%)
  local copies, waits for them, and re-layouts  90.4 us (10%)
  matrix products  48.7 us (5%)
  starting transfers between devices  47.2 us (5%)
    ppermute x3, waiting for transfers between devices, from_partner(): return lax.ppermute(block, axis, route)  292 us
    all_to_all x2, waiting for transfers between devices, body(): lax.all_to_all(outgoing, 'ep', split_axis=0, concat_axis=0, tiled=True)  281 us
    all_to_all x2, waiting for transfers between devices, serve_rows(): lax.all_to_all(produced, 'ep', split_axis=0, concat_axis=0, tiled=True)  144 us
    scatter x2, local copies, waits for them, and re-layouts, body(): packed = jnp.zeros((positions * capacity, model_width), jnp.bfloat16).at[...  33.1 us
    dot_general x2, matrix products, expert_rows(): jnp.dot(hidden, down_mat, preferred_element_type=jnp.float32)  23.1 us
    all_to_all x2, starting transfers between devices, body(): lax.all_to_all(outgoing, 'ep', split_axis=0, concat_axis=0, tiled=True)  21.8 us
    all_to_all x2, starting transfers between devices, serve_rows(): lax.all_to_all(produced, 'ep', split_axis=0, concat_axis=0, tiled=True)  21 us
  transfers between devices with their start and end apart: 7, of which 6 were waited for; matrix products, arithmetic and copies ran while one was open for 10% of the time, Pallas kernels for 0%

commit v1 on v0

v1 whole, which is shorter than its diff:
```python
import jax
import jax.numpy as jnp
from jax import lax
from jax.sharding import PartitionSpec as P

CAP = 8
BF16 = jnp.bfloat16
F32 = jnp.float32


def plan(experts, gates, chosen_by, layout, allowed):
    hit = (experts[:, :, None] == layout[None, None, :]) & allowed[chosen_by][:, None, :]
    named = jnp.any(hit, axis=1)
    weight = jnp.sum(jnp.where(hit, gates[:, :, None], 0.0), axis=1)
    tokens = experts.shape[0]
    before = jnp.tril(jnp.ones((tokens, tokens), BF16), -1)
    rank = jnp.dot(before, named.astype(BF16), preferred_element_type=F32).astype(jnp.int32)
    in_slot = named[:, :, None] & (rank[:, :, None] == jnp.arange(CAP, dtype=jnp.int32))
    positions = layout.shape[0]
    pick = in_slot.reshape(tokens, positions * CAP).astype(BF16)
    mix = jnp.where(in_slot, weight[:, :, None], 0.0).reshape(tokens, positions * CAP)
    return pick, mix


def ffn(rows, halves):
    total = None
    for gate_mat, up_mat, down_mat in halves:
        gate_part = jnp.dot(rows, gate_mat, preferred_element_type=F32)
        up_part = jnp.dot(rows, up_mat, preferred_element_type=F32)
        hidden = (jax.nn.silu(gate_part) * up_part).astype(BF16)
        part = jnp.dot(hidden, down_mat, preferred_element_type=F32)
        total = part if total is None else total + part
    return total.astype(BF16)


def body(tokens, routing, route_gate, place_old, place_new, gate_proj, up_proj, down_proj):
    ep_count = lax.axis_size("ep")
    positions = ep_count // 2
    rep = lax.axis_index("rep")
    batches, rows, width = tokens.shape
    groups = [[2 * e + c for e in range(positions)] for c in range(2)]
    swap_core = [(i, i ^ 1) for i in range(ep_count)]
    swap_rep = [(0, 1), (1, 0)]
    own = (gate_proj[0, 0], up_proj[0, 0], down_proj[0, 0])
    other = tuple(lax.ppermute(w, "ep", swap_core) for w in own)
    layout = lax.dynamic_index_in_dim(place_old, rep, 0, keepdims=False)
    moved = lax.dynamic_index_in_dim(place_new, rep, 0, keepdims=False) != layout

    their_tokens = lax.ppermute(tokens[1], "rep", swap_rep)
    their_routing = lax.ppermute(routing[1], "rep", swap_rep)
    their_gate = lax.ppermute(route_gate[1], "rep", swap_rep)

    mine = jnp.zeros((rows,), jnp.int32)
    anywhere = jnp.ones((1, positions), bool)
    plans = [
        plan(routing[0], route_gate[0], mine, layout, anywhere),
        plan(
            jnp.concatenate([routing[1], their_routing]),
            jnp.concatenate([route_gate[1], their_gate]),
            jnp.concatenate([mine, mine + 1]),
            layout,
            jnp.stack([~moved, moved]),
        ),
    ]
    sources = [tokens[0], jnp.concatenate([tokens[1], their_tokens])]

    def a2a(x):
        return lax.all_to_all(x, "ep", split_axis=0, concat_axis=0, axis_index_groups=groups, tiled=True)

    outs = []
    for (pick, mix), source in zip(plans, sources):
        packed = lax.dot_general(pick, source, (((0,), (0,)), ((), ())), preferred_element_type=F32).astype(BF16)
        received = a2a(packed.reshape(positions, CAP, width))
        produced = ffn(received.reshape(positions * CAP, width), (own, other))
        back = a2a(produced.reshape(positions, CAP, width)).reshape(positions * CAP, width)
        high = mix.astype(BF16)
        low = (mix - high.astype(F32)).astype(BF16)
        both = jnp.dot(jnp.concatenate([high, low]), back, preferred_element_type=F32)
        outs.append(both[: mix.shape[0]] + both[mix.shape[0] :])
    returned = lax.ppermute(outs[1][rows:].astype(BF16), "rep", swap_rep)
    second = outs[1][:rows] + returned.astype(F32)
    return jnp.stack([outs[0].astype(BF16), second.astype(BF16)])


def solution(mesh):
    return jax.shard_map(
        body,
        mesh=mesh,
        in_specs=(
            P(None, ("rep", "ep"), None),
            P(None, ("rep", "ep"), None),
            P(None, ("rep", "ep"), None),
            P(),
            P(),
            P("rep", "ep", None, None),
            P("rep", "ep", None, None),
            P("rep", "ep", None, None),
        ),
        out_specs=P(None, ("rep", "ep"), None),
        check_vma=False,
    )
```

time: 922 us -> 389 us (0.42)
  waiting for transfers between devices: 717 us -> 264 us
  local copies, waits for them, and re-layouts: 90.4 us -> 5.21 us
  matrix products: 48.7 us -> 78.4 us
  starting transfers between devices: 47.2 us -> 37.4 us
    ppermute x3 -> x7, waiting for transfers between devices: 292 us -> 26.6 us  [the longest x1 6.68 us: body(): returned = lax.ppermute(outs[1][rows:].astype(BF16), 'rep', swap_rep)]
    all_to_all x4, waiting for transfers between devices: 425 us -> 238 us  [a2a(): lax.all_to_all(x, 'ep', split_axis=0, concat_axis=0, axis_index_groups=gr...]
    scatter x2 -> x0, local copies, waits for them, and re-layouts: 33.1 us -> none  [body(): packed = jnp.zeros((positions * capacity, model_width), jnp.bfloat16).at[...]
    dot_general x5 -> x14, matrix products: 48.7 us -> 78.4 us  [the longest x4 46.8 us: ffn(): part = jnp.dot(hidden, down_mat, preferred_element_type=F32)]
    gather x4 -> x1, local copies, waits for them, and re-layouts: 28.3 us -> 0.63 us  [plan(): allowed[chosen_by][:, None, :]]
    another operation x5 -> x0, local copies, waits for them, and re-layouts: 13.3 us -> none  [the longest x2 13.1 us: body(): first = halves[:, 0].reshape(positions * capacity, model_width)[slot_index]]
    all_to_all x4, starting transfers between devices: 42.8 us -> 31.2 us  [a2a(): lax.all_to_all(x, 'ep', split_axis=0, concat_axis=0, axis_index_groups=gr...]
    broadcast_in_dim x2 -> x4, local copies, waits for them, and re-layouts: 11.2 us -> 0.2 us  [the longest x2 0.12 us: plan(): jnp.where(in_slot, weight[:, :, None], 0.0).reshape(tokens, positions * CAP)]
  transfers between devices with their start and end apart: 7 -> 11, of which waited for: 6 -> 9; matrix products, arithmetic and copies ran while one was open for 10% -> 19% of each run, Pallas kernels for 0% -> 0%
where the time goes in v1:
time: 389 us; the launch traced here: 388 us
  waiting for transfers between devices  264 us (68%)
  matrix products  78.4 us (20%)
  starting transfers between devices  37.4 us (10%)
  local copies, waits for them, and re-layouts  5.21 us (1%)
    all_to_all x4, waiting for transfers between devices, a2a(): lax.all_to_all(x, 'ep', split_axis=0, concat_axis=0, axis_index_groups=gr...  238 us
    dot_general x4, matrix products, ffn(): part = jnp.dot(hidden, down_mat, preferred_element_type=F32)  46.8 us
    all_to_all x4, starting transfers between devices, a2a(): lax.all_to_all(x, 'ep', split_axis=0, concat_axis=0, axis_index_groups=gr...  31.2 us
    dot_general x2, matrix products, ffn(): gate_part = jnp.dot(rows, gate_mat, preferred_element_type=F32)  10.6 us
    dot_general x2, matrix products, ffn(): up_part = jnp.dot(rows, up_mat, preferred_element_type=F32)  8.18 us
  transfers between devices with their start and end apart: 11, of which 9 were waited for; matrix products, arithmetic and copies ran while one was open for 19% of the time, Pallas kernels for 0%

profile of v1, /device:TPU:4, one launch (start us, length us, event | category | flops | bytes accessed | tf_op | source)
XLA Modules:
  0.0 387.9 jit_solution(4455574444835609)
XLA Ops:
  0.0 0.7 slice_bitcast_fusion.4
  0.7 0.1 copy.29
  0.8 0.7 fusion.95
  1.5 0.1 compare_reduce_fusion
  1.6 0.1 copy.30
  1.7 0.2 convolution_convert_fusion.3
  1.9 0.1 copy.31
  2.0 3.9 fusion
  5.8 13.1 %all-to-all-start = ((bf16[64,8,3584]{2,1,0:T(8,128)(2,1)}), bf16[64,8,3584]{2,1,0:T(8,128)(2,1)}, u32[]{:S(2)}, u32[]{:S(2)}) async-start(bf16[64,8,3584]{2,1,0:T(8,128)(2,1)} %fusion), calls=%async_computation | async-start | bytes 7340032 | tf_op jit(solution)/shard_map/all_to_all | solution.py:68
  19.0 0.9 collective-permute-start.3
  19.9 2.8 collective-permute-start.5
  22.8 0.1 eq.91
  22.9 0.6 gather_fusion
  23.5 4.9 %collective-permute-done.3 = s32[32,8]{0,1:T(8,128)S(1)} collective-permute-done((s32[32,8]{0,1:T(8,128)S(1)}, s32[32,8]{0,1:T(8,128)S(1)}, u32[]{:S(2)}, u32[]{:S(2)}) %collective-permute-start.3) | collective-permute-done | bytes 1056 | tf_op jit(solution)/shard_map/ppermute | solution.py:50
  28.4 0.1 pad_add_fusion
  28.5 0.1 copy.37
  28.6 0.2 fusion.67
  28.7 0.1 copy.38
  28.8 0.2 convolution_convert_fusion.2
  29.0 0.1 copy.39
  29.1 4.3 %collective-permute-done.5 = bf16[32,3584]{1,0:T(8,128)(2,1)S(1)} collective-permute-done((bf16[32,3584]{1,0:T(8,128)(2,1)S(1)}, bf16[32,3584]{1,0:T(8,128)(2,1)S(1)}, u32[]{:S(2)}, u32[]{:S(2)}) %collective-permute-start.5) | collective-permute-done | bytes 229408 | tf_op jit(solution)/shard_map/ppermute | solution.py:49
  33.5 3.0 fusion.1
  36.5 67.3 %all-to-all-done = bf16[64,8,3584]{2,1,0:T(8,128)(2,1)} async-done(((bf16[64,8,3584]{2,1,0:T(8,128)(2,1)}), bf16[64,8,3584]{2,1,0:T(8,128)(2,1)}, u32[]{:S(2)}, u32[]{:S(2)}) %all-to-all-start) | async-done | bytes 3670048 | tf_op jit(solution)/shard_map/all_to_all | solution.py:68
  103.8 6.4 %all-to-all-start.2 = ((bf16[64,8,3584]{2,1,0:T(8,128)(2,1)}), bf16[64,8,3584]{2,1,0:T(8,128)(2,1)}, u32[]{:S(2)}, u32[]{:S(2)}) async-start(bf16[64,8,3584]{2,1,0:T(8,128)(2,1)} %fusion.1), calls=%async_computation.2 | async-start | bytes 7340032 | tf_op jit(solution)/shard_map/all_to_all | solution.py:68
  110.1 0.1 collective-permute-start.1
  110.2 0.5 collective-permute-start
  110.7 0.1 collective-permute-start.2
  110.8 5.2 %fusion.22 = f32[512,512]{1,0:T(8,128)S(1)} fusion(bf16[64,8,3584]{2,1,0:T(8,128)(2,1)} %all-to-all-done, bf16[1,1,3584,512]{3,2,1,0:T(8,128)(2,1)} %param.13), kind=kOutput, calls=%fused_computation.27 | convolution fusion | flops 1879048192 | bytes 8388608 | tf_op jit(solution)/shard_map/dot_general | solution.py:28
  116.1 5.0 %collective-permute-done.1 = bf16[3584,512]{1,0:T(8,128)(2,1)S(1)} collective-permute-done((bf16[3584,512]{1,0:T(8,128)(2,1)}, bf16[3584,512]{1,0:T(8,128)(2,1)S(1)}, u32[]{:S(2)}, u32[]{:S(2)}) %collective-permute-start.1) | collective-permute-done | bytes 3670048 | tf_op jit(solution)/shard_map/ppermute | solution.py:45
  121.1 1.8 copy-done.5
  122.9 4.1 %fusion.16 = f32[512,512]{1,0:T(8,128)S(1)} fusion(bf16[3584,512]{1,0:T(8,128)(2,1)S(1)} %collective-permute-done.1, bf16[64,8,3584]{2,1,0:T(8,128)(2,1)} %all-to-all-done), kind=kOutput, calls=%fused_computation.21 | convolution fusion | flops 1879048192 | bytes 8388608 | tf_op jit(solution)/shard_map/dot_general | solution.py:29
  127.0 11.2 %fusion.37 = f32[512,3584]{1,0:T(8,128)} fusion(bf16[64,8,3584]{2,1,0:T(8,128)(2,1)} %all-to-all-done, f32[512,512]{1,0:T(8,128)S(1)} %fusion.22, bf16[1,1,512,3584]{3,2,1,0:T(8,128)(2,1)} %param.15, bf16[1,1,3584,512]{3,2,1,0:T(8,128)(2,1)} %param.14), kind=kOutput, calls=%fused_computation.38 | convolution fusion | flops 3759669248 | bytes 19398656 | tf_op jit(solution)/shard_map/dot_general | solution.py:31
  138.1 0.0 collective-permute-done
  138.1 12.2 %fusion.2 = bf16[64,8,3584]{2,1,0:T(8,128)(2,1)} fusion(f32[512,3584]{1,0:T(8,128)} %fusion.37, bf16[512,3584]{1,0:T(8,128)(2,1)} %collective-permute-done.2, f32[512,512]{1,0:T(8,128)S(1)} %fusion.16, bf16[3584,512]{1,0:T(8,128)(2,1)} %collective-permute-done, bf16[64,8,3584]{2,1,0:T(8,128)(2,1)} %all-to-all-done), kind=kOutput, calls=%fused_computation.7 | convolution fusion | flops 3763339264 | bytes 23068672 | tf_op jit(solution)/shard_map/dot_general | solution.py:31
  150.4 44.7 %all-to-all-done.2 = bf16[64,8,3584]{2,1,0:T(8,128)(2,1)} async-done(((bf16[64,8,3584]{2,1,0:T(8,128)(2,1)}), bf16[64,8,3584]{2,1,0:T(8,128)(2,1)}, u32[]{:S(2)}, u32[]{:S(2)}) %all-to-all-start.2) | async-done | bytes 3670048 | tf_op jit(solution)/shard_map/all_to_all | solution.py:68
  195.1 6.0 %all-to-all-start.1 = ((bf16[64,8,3584]{2,1,0:T(8,128)(2,1)}), bf16[64,8,3584]{2,1,0:T(8,128)(2,1)}, u32[]{:S(2)}, u32[]{:S(2)}) async-start(bf16[64,8,3584]{2,1,0:T(8,128)(2,1)} %fusion.2), calls=%async_computation.1 | async-start | bytes 7340032 | tf_op jit(solution)/shard_map/all_to_all | solution.py:68
  201.1 5.3 %fusion.12 = f32[512,512]{1,0:T(8,128)S(1)} fusion(bf16[64,8,3584]{2,1,0:T(8,128)(2,1)} %all-to-all-done.2, bf16[1,1,3584,512]{3,2,1,0:T(8,128)(2,1)} %param.13), kind=kOutput, calls=%fused_computation.17 | convolution fusion | flops 1879048192 | bytes 8388608 | tf_op jit(solution)/shard_map/dot_general | solution.py:28
  206.4 4.1 %fusion.6 = f32[512,512]{1,0:T(8,128)S(1)} fusion(bf16[3584,512]{1,0:T(8,128)(2,1)S(1)} %copy-done.6, bf16[64,8,3584]{2,1,0:T(8,128)(2,1)} %all-to-all-done.2), kind=kOutput, calls=%fused_computation.11 | convolution fusion | flops 1879048192 | bytes 8388608 | tf_op jit(solution)/shard_map/dot_general | solution.py:29
  210.5 11.2 %fusion.40 = f32[512,3584]{1,0:T(8,128)} fusion(bf16[64,8,3584]{2,1,0:T(8,128)(2,1)} %all-to-all-done.2, f32[512,512]{1,0:T(8,128)S(1)} %fusion.12, bf16[1,1,512,3584]{3,2,1,0:T(8,128)(2,1)} %param.15, bf16[1,1,3584,512]{3,2,1,0:T(8,128)(2,1)} %param.14), kind=kOutput, calls=%fused_computation.39 | convolution fusion | flops 3759669248 | bytes 19398656 | tf_op jit(solution)/shard_map/dot_general | solution.py:31
  221.7 12.2 %fusion.3 = bf16[64,8,3584]{2,1,0:T(8,128)(2,1)} fusion(f32[512,3584]{1,0:T(8,128)} %fusion.40, bf16[512,3584]{1,0:T(8,128)(2,1)} %collective-permute-done.2, f32[512,512]{1,0:T(8,128)S(1)} %fusion.6, bf16[3584,512]{1,0:T(8,128)(2,1)} %collective-permute-done, bf16[64,8,3584]{2,1,0:T(8,128)(2,1)} %all-to-all-done.2), kind=kOutput, calls=%fused_computation.8 | convolution fusion | flops 3763339264 | bytes 23068672 | tf_op jit(solution)/shard_map/dot_general | solution.py:31
  233.9 51.8 %all-to-all-done.1 = bf16[64,8,3584]{2,1,0:T(8,128)(2,1)} async-done(((bf16[64,8,3584]{2,1,0:T(8,128)(2,1)}), bf16[64,8,3584]{2,1,0:T(8,128)(2,1)}, u32[]{:S(2)}, u32[]{:S(2)}) %all-to-all-start.1) | async-done | bytes 3670048 | tf_op jit(solution)/shard_map/all_to_all | solution.py:68
  285.8 5.8 %all-to-all-start.3 = ((bf16[64,8,3584]{2,1,0:T(8,128)(2,1)}), bf16[64,8,3584]{2,1,0:T(8,128)(2,1)}, u32[]{:S(2)}, u32[]{:S(2)}) async-start(bf16[64,8,3584]{2,1,0:T(8,128)(2,1)} %fusion.3), calls=%async_computation.3 | async-start | bytes 7340032 | tf_op jit(solution)/shard_map/all_to_all | solution.py:68
  291.6 0.9 collective-permute-start.4
  292.5 0.1 copy.32
  292.6 0.1 copy.33
  292.8 0.1 copy.34
  292.8 0.1 fusion.72
  293.0 0.1 copy.35
  293.1 0.1 copy.36
  293.3 5.7 %collective-permute-done.4 = f32[32,8]{0,1:T(8,128)S(1)} collective-permute-done((f32[32,8]{0,1:T(8,128)S(1)}, f32[32,8]{0,1:T(8,128)S(1)}, u32[]{:S(2)}, u32[]{:S(2)}) %collective-permute-start.4) | collective-permute-done | bytes 1056 | tf_op jit(solution)/shard_map/ppermute | solution.py:51
  298.9 0.1 pad_maximum_fusion.1
  299.0 0.1 copy.40
  299.1 0.2 select_reduce_fusion
  299.3 0.1 copy.41
  299.4 0.1 fusion.60
  299.5 0.1 fusion.61
  299.7 2.8 fusion.14
  302.5 74.0 %all-to-all-done.3 = bf16[64,8,3584]{2,1,0:T(8,128)(2,1)} async-done(((bf16[64,8,3584]{2,1,0:T(8,128)(2,1)}), bf16[64,8,3584]{2,1,0:T(8,128)(2,1)}, u32[]{:S(2)}, u32[]{:S(2)}) %all-to-all-start.3) | async-done | bytes 3670048 | tf_op jit(solution)/shard_map/all_to_all | solution.py:68
  376.5 2.8 fusion.4
  379.3 0.1 slice_add_fusion
  379.4 0.9 collective-permute-start.6
  380.3 6.7 %collective-permute-done.6 = bf16[32,3584]{1,0:T(8,128)(2,1)S(1)} collective-permute-done((bf16[32,3584]{1,0:T(8,128)(2,1)S(1)}, bf16[32,3584]{1,0:T(8,128)(2,1)S(1)}, u32[]{:S(2)}, u32[]{:S(2)}) %collective-permute-start.6) | collective-permute-done | bytes 229408 | tf_op jit(solution)/shard_map/ppermute | solution.py:80
  387.0 0.1 fusion.69
  387.1 0.8 pad_maximum_fusion
  (29 shorter events, 0.3 us)
Async XLA Ops:
  5.8 14.0 %copy-start = (bf16[2,32,3584]{2,1,0:T(8,128)(2,1)S(1)}, bf16[2,32,3584]{2,1,0:T(8,128)(2,1)}, u32[]{:S(2)}) copy-start(bf16[2,32,3584]{2,1,0:T(8,128)(2,1)} %param.8) | copy-start | bytes 1376260
  5.8 16.9 %copy-start.3 = (s32[2,64]{1,0:T(2,128)S(1)}, s32[2,64]{1,0:T(2,128)}, u32[]{:S(2)}) copy-start(s32[2,64]{1,0:T(2,128)} %param.11) | copy-start | bytes 1540
  5.8 16.9 %copy-start.4 = (s32[2,64]{1,0:T(2,128)S(1)}, s32[2,64]{1,0:T(2,128)}, u32[]{:S(2)}) copy-start(s32[2,64]{1,0:T(2,128)} %param.12) | copy-start | bytes 1540
  5.8 16.9 %copy-start.2 = (s32[64]{0:T(128)S(1)}, s32[64]{0:T(128)}, u32[]{:S(2)}) copy-start(s32[64]{0:T(128)} %constant.48) | copy-start | bytes 772
  5.8 97.9 %all-to-all-start = ((bf16[64,8,3584]{2,1,0:T(8,128)(2,1)}), bf16[64,8,3584]{2,1,0:T(8,128)(2,1)}, u32[]{:S(2)}, u32[]{:S(2)}) async-start(bf16[64,8,3584]{2,1,0:T(8,128)(2,1)} %fusion), calls=%async_computation | async-start | bytes 7340032 | tf_op jit(solution)/shard_map/all_to_all | solution.py:68
  19.0 9.4 %collective-permute-start.3 = (s32[32,8]{0,1:T(8,128)S(1)}, s32[32,8]{0,1:T(8,128)S(1)}, u32[]{:S(2)}, u32[]{:S(2)}) collective-permute-start(s32[32,8]{0,1:T(8,128)S(1)} %get-tuple-element.10), channel_id=1, source_target_pairs={{0,128},{128,0},{1,129},{129,1},{2,130},{130,2},{3,131},{131,3},{4... | collective-permute-start | bytes 3080 | tf_op jit(solution)/shard_map/ppermute | solution.py:50
  19.9 13.6 %collective-permute-start.5 = (bf16[32,3584]{1,0:T(8,128)(2,1)S(1)}, bf16[32,3584]{1,0:T(8,128)(2,1)S(1)}, u32[]{:S(2)}, u32[]{:S(2)}) collective-permute-start(bf16[32,3584]{1,0:T(8,128)(2,1)S(1)} %slice_bitcast_fusion), channel_id=1, source_target_pairs={{0,128},{128,0},{1,129},{129,1},{2,130},{130,2},{3,131},{131,3},{4... | collective-permute-start | bytes 688136 | tf_op jit(solution)/shard_map/ppermute | solution.py:49
  103.8 91.3 %all-to-all-start.2 = ((bf16[64,8,3584]{2,1,0:T(8,128)(2,1)}), bf16[64,8,3584]{2,1,0:T(8,128)(2,1)}, u32[]{:S(2)}, u32[]{:S(2)}) async-start(bf16[64,8,3584]{2,1,0:T(8,128)(2,1)} %fusion.1), calls=%async_computation.2 | async-start | bytes 7340032 | tf_op jit(solution)/shard_map/all_to_all | solution.py:68
  110.1 10.9 %collective-permute-start.1 = (bf16[3584,512]{1,0:T(8,128)(2,1)}, bf16[3584,512]{1,0:T(8,128)(2,1)S(1)}, u32[]{:S(2)}, u32[]{:S(2)}) collective-permute-start(bf16[3584,512]{1,0:T(8,128)(2,1)} %bitcast.137), channel_id=1, source_target_pairs={{0,1},{1,0},{2,3},{3,2},{4,5},{5,4},{6,7},{7,6},{8,9},{9,8},{10,11... | collective-permute-start | bytes 11010056 | tf_op jit(solution)/shard_map/ppermute | solution.py:45
  110.2 27.9 %collective-permute-start = (bf16[3584,512]{1,0:T(8,128)(2,1)}, bf16[3584,512]{1,0:T(8,128)(2,1)}, u32[]{:S(2)}, u32[]{:S(2)}) collective-permute-start(bf16[3584,512]{1,0:T(8,128)(2,1)} %bitcast.135), channel_id=1, source_target_pairs={{0,1},{1,0},{2,3},{3,2},{4,5},{5,4},{6,7},{7,6},{8,9},{9,8},{10,11... | collective-permute-start | bytes 11010056 | tf_op jit(solution)/shard_map/ppermute | solution.py:45
  110.7 27.4 %collective-permute-start.2 = (bf16[512,3584]{1,0:T(8,128)(2,1)}, bf16[512,3584]{1,0:T(8,128)(2,1)}, u32[]{:S(2)}, u32[]{:S(2)}) collective-permute-start(bf16[512,3584]{1,0:T(8,128)(2,1)} %bitcast.136), channel_id=1, source_target_pairs={{0,1},{1,0},{2,3},{3,2},{4,5},{5,4},{6,7},{7,6},{8,9},{9,8},{10,11... | collective-permute-start | bytes 11010056 | tf_op jit(solution)/shard_map/ppermute | solution.py:45
  121.1 1.8 copy-start.5
  195.1 90.7 %all-to-all-start.1 = ((bf16[64,8,3584]{2,1,0:T(8,128)(2,1)}), bf16[64,8,3584]{2,1,0:T(8,128)(2,1)}, u32[]{:S(2)}, u32[]{:S(2)}) async-start(bf16[64,8,3584]{2,1,0:T(8,128)(2,1)} %fusion.2), calls=%async_computation.1 | async-start | bytes 7340032 | tf_op jit(solution)/shard_map/all_to_all | solution.py:68
  201.1 5.4 %copy-start.6 = (bf16[3584,512]{1,0:T(8,128)(2,1)S(1)}, bf16[3584,512]{1,0:T(8,128)(2,1)}, u32[]{:S(2)}) copy-start(bf16[3584,512]{1,0:T(8,128)(2,1)} %copy-done.5) | copy-start | bytes 11010052
  233.9 57.6 %copy-start.1 = (f32[2,32,8]{1,2,0:T(8,128)S(1)}, f32[2,32,8]{1,2,0:T(8,128)}, u32[]{:S(2)}) copy-start(f32[2,32,8]{1,2,0:T(8,128)} %param.10) | copy-start | bytes 6148
  285.8 90.7 %all-to-all-start.3 = ((bf16[64,8,3584]{2,1,0:T(8,128)(2,1)}), bf16[64,8,3584]{2,1,0:T(8,128)(2,1)}, u32[]{:S(2)}, u32[]{:S(2)}) async-start(bf16[64,8,3584]{2,1,0:T(8,128)(2,1)} %fusion.3), calls=%async_computation.3 | async-start | bytes 7340032 | tf_op jit(solution)/shard_map/all_to_all | solution.py:68
  291.6 7.4 %collective-permute-start.4 = (f32[32,8]{0,1:T(8,128)S(1)}, f32[32,8]{0,1:T(8,128)S(1)}, u32[]{:S(2)}, u32[]{:S(2)}) collective-permute-start(f32[32,8]{0,1:T(8,128)S(1)} %get-tuple-element.8), channel_id=1, source_target_pairs={{0,128},{128,0},{1,129},{129,1},{2,130},{130,2},{3,131},{131,3},{4... | collective-permute-start | bytes 3080 | tf_op jit(solution)/shard_map/ppermute | solution.py:51
  379.4 7.6 %collective-permute-start.6 = (bf16[32,3584]{1,0:T(8,128)(2,1)S(1)}, bf16[32,3584]{1,0:T(8,128)(2,1)S(1)}, u32[]{:S(2)}, u32[]{:S(2)}) collective-permute-start(bf16[32,3584]{1,0:T(8,128)(2,1)S(1)} %slice.85), channel_id=1, source_target_pairs={{0,128},{128,0},{1,129},{129,1},{2,130},{130,2},{3,131},{131,3},{4... | collective-permute-start | bytes 688136 | tf_op jit(solution)/shard_map/ppermute | solution.py:80

commit v2 on v1

v2 whole, which is shorter than its diff:
```python
import jax
import jax.numpy as jnp
from jax import lax
from jax.experimental import pallas as pl
from jax.experimental.pallas import tpu as pltpu
from jax.sharding import PartitionSpec as P

CAP = 8
BF16 = jnp.bfloat16
F32 = jnp.float32
NY, NZ, NX = 4, 8, 2
PLANE = NY * NX
PAIRS = 4
UNIT = 2 * CAP
META = NZ * 32
MESH = pl.DeviceIdType.MESH
MIB = 1 << 20


def token_block(tokens, experts, gates, layout, allowed):
    hit = (experts[:, :, None] == layout[None, None, :]) & allowed[None, None, :]
    named = jnp.any(hit, axis=1)
    weight = jnp.sum(jnp.where(hit, gates[:, :, None], 0.0), axis=1)
    count = experts.shape[0]
    before = jnp.tril(jnp.ones((count, count), BF16), -1)
    rank = jnp.dot(before, named.astype(BF16), preferred_element_type=F32)
    rank = jnp.where(named, rank, -1.0).astype(BF16)
    high = lax.reduce_precision(weight, 8, 7)
    low = (weight - high).astype(BF16)
    kinds = jnp.stack([rank, high.astype(BF16), low, jnp.zeros_like(rank)], axis=1)
    kinds = kinds.reshape(count, 4, NY, NZ, NX).transpose(0, 3, 1, 2, 4)
    return jnp.concatenate([tokens, kinds.reshape(count, META)], axis=1)


def kernel(
    tb0, tb1, tbx, gate_hbm, up_hbm, down_hbm, out,
    wg, wu, wd, g0, g1, s0, s1, r0, r1, t0, t1, q0, q1, w0, w1, acc0, acc1, hid, sel, swap,
    load_sem, wsend, wrecv, own_sem, xsend, xrecv,
    gsend, grecv, dsend, drecv, dloc, csend, crecv, cloc, rsend, rrecv,
):
    width = out.shape[2]
    half = width // 2
    ghalf = (width + META) // 2
    tile = 512
    rep = lax.axis_index("rep")
    ep = lax.axis_index("ep")
    core = lax.rem(ep, 2)
    x = lax.rem(lax.div(ep, 2), NX)
    z = lax.rem(lax.div(ep, 2 * NX), NZ)
    y = lax.div(ep, 2 * NX * NZ)
    here = y * NX + x

    def at(yy, zz, xx):
        return (rep, ((yy * NZ + zz) * NX + xx) * 2 + core)

    right = at(y, lax.rem(z + 1, NZ), x)
    left = at(y, lax.rem(z + NZ - 1, NZ), x)
    other_rep = (1 - rep, ep)
    other_core = (rep, ep + 1 - 2 * core)
    plane = []
    for d in range(1, PLANE):
        yy, xx = lax.rem(y + d // NX, NY), lax.rem(x + d % NX, NX)
        plane.append((yy * NX + xx, at(yy, z, xx)))

    barrier = pltpu.get_barrier_semaphore()
    partners = [right, left, other_rep, other_core] + [dev for _, dev in plane]
    for dev in partners:
        pl.semaphore_signal(barrier, inc=1, device_id=dev, device_id_type=MESH)
    pl.semaphore_wait(barrier, len(partners))

    def remote(src, dst, send, recv, dev):
        return pltpu.make_async_remote_copy(
            src_ref=src, dst_ref=dst, send_sem=send, recv_sem=recv, device_id=dev, device_id_type=MESH
        )

    def unit(p, j):
        return pl.ds(pl.multiple_of(j * PLANE * UNIT + p * UNIT, UNIT), UNIT)

    rows_of = (32, 64)
    G, S, R, T, Q, W, ACC = (g0, g1), (s0, s1), (r0, r1), (t0, t1), (q0, q1), (w0, w1), (acc0, acc1)

    def ring_out(b, k):
        n = rows_of[b]
        g = G[b]
        first, second = pl.ds(0, n), pl.ds(n, n)
        if k == 1:
            src_r, src_l = g.at[3, first], g.at[3, first]
        elif k < 4:
            src_r, src_l = g.at[k - 2, first], g.at[k - 2, second]
        else:
            src_r = g.at[2, first, pl.ds(0, ghalf)]
            src_l = g.at[2, second, pl.ds(ghalf, ghalf)]
        if k < 4:
            dst_r, dst_l = g.at[k - 1, first], g.at[k - 1, second]
        else:
            dst_r = g.at[3, second, pl.ds(0, ghalf)]
            dst_l = g.at[3, second, pl.ds(ghalf, ghalf)]
        return (
            remote(src_r, dst_r, gsend.at[b, k - 1, 0], grecv.at[b, k - 1, 0], right),
            remote(src_l, dst_l, gsend.at[b, k - 1, 1], grecv.at[b, k - 1, 1], left),
        )

    def ring_start(b, k):
        for copy in ring_out(b, k):
            copy.start()

    def dispatch_copies(b, j):
        remotes = [
            remote(S[b].at[unit(p, j)], R[b].at[unit(here, j)], dsend.at[b, j, d], drecv.at[b, j, d], dev)
            for d, (p, dev) in enumerate(plane)
        ]
        return remotes, pltpu.make_async_copy(S[b].at[unit(here, j)], R[b].at[unit(here, j)], dloc.at[b, j])

    def pack(b, j):
        n = rows_of[b]
        g, s, w = G[b], S[b], W[b]
        meta = jnp.dot(g[j, :, width:], sel[...], preferred_element_type=F32)
        lane = lax.broadcasted_iota(jnp.int32, (2 * n, 128), 1)
        row = lax.broadcasted_iota(jnp.int32, (2 * n, 128), 0)
        fits = (meta[:, :128] == (lane & 7).astype(F32)) & (((lane >> 3) & 1) == (row >= n).astype(jnp.int32))
        w[j, : 2 * n] = jnp.where(fits, meta[:, 128:256], 0.0).astype(BF16)
        w[j, 2 * n :] = jnp.where(fits, meta[:, 256:], 0.0).astype(BF16)
        pick = jnp.where(fits, 1.0, 0.0).T.astype(BF16)

        @pl.loop(0, width // tile)
        def _(i):
            cols = pl.ds(pl.multiple_of(i * tile, tile), tile)
            s[pl.ds(j * PLANE * UNIT, PLANE * UNIT), cols] = jnp.dot(
                pick, g[j, :, cols], preferred_element_type=F32
            ).astype(BF16)

        remotes, local = dispatch_copies(b, j)
        for copy in remotes:
            copy.start()
        local.start()

    def dispatch_wait(b, j):
        remotes, local = dispatch_copies(b, j)
        for copy in remotes:
            copy.wait_recv()
        local.wait()

    def gather_step(b, k):
        for copy in ring_out(b, k):
            copy.wait_recv()
        if k < 4:
            ring_start(b, k + 1)

    def ffn(b, m):
        rows = pl.ds(m * 256, 256)
        r = R[b]

        @pl.loop(0, 4)
        def _(i):
            h = lax.div(i, 2)
            cols = pl.ds(pl.multiple_of(lax.rem(i, 2) * 256, 256), 256)
            gate = jnp.dot(r[rows, :], wg[h, :, cols], preferred_element_type=F32)
            up = jnp.dot(r[rows, :], wu[h, :, cols], preferred_element_type=F32)
            hid[:, pl.ds(pl.multiple_of(i * 256, 256), 256)] = (jax.nn.silu(gate) * up).astype(BF16)

        @pl.loop(0, width // tile)
        def _(i):
            cols = pl.ds(pl.multiple_of(i * tile, tile), tile)
            down = jnp.dot(hid[:, :512], wd[0, :, cols], preferred_element_type=F32)
            down = down + jnp.dot(hid[:, 512:], wd[1, :, cols], preferred_element_type=F32)
            r[rows, cols] = down.astype(BF16)

    def return_copies(b, j):
        remotes = [
            remote(R[b].at[unit(p, j)], T[b].at[unit(here, j)], csend.at[b, j, d], crecv.at[b, j, d], dev)
            for d, (p, dev) in enumerate(plane)
        ]
        return remotes, pltpu.make_async_copy(R[b].at[unit(here, j)], T[b].at[unit(here, j)], cloc.at[b, j])

    def give_back(b, j):
        remotes, local = return_copies(b, j)
        for copy in remotes:
            copy.start()
        local.start()

    def sum_out(b, k):
        q = Q[b]
        lo, hi = pl.ds(0, half), pl.ds(half, half)
        if k == 4:
            pairs = ((q.at[8, :, lo], q.at[3, :, lo]), (q.at[8, :, hi], q.at[7, :, hi]))
        else:
            pairs = ((q.at[k], q.at[k - 1]), (q.at[4 + k], q.at[3 + k]))
        return tuple(
            remote(src, dst, rsend.at[b, k - 1, i], rrecv.at[b, k - 1, i], dev)
            for i, ((src, dst), dev) in enumerate(zip(pairs, (right, left)))
        )

    def combine_step(b, k):
        n = rows_of[b]
        q, t, w = Q[b], T[b], W[b]
        j = k - 1
        remotes, local = return_copies(b, j)
        for copy in remotes:
            copy.wait_recv()
        local.wait()
        if k < 4:
            for copy in sum_out(b, k + 1):
                copy.wait_recv()
        for first in range(0, width, half):

            @pl.loop(0, half // 256)
            def _(i):
                cols = pl.ds(pl.multiple_of(first + i * 256, 256), 256)
                both = jnp.dot(
                    w[j], t[pl.ds(j * PLANE * UNIT, PLANE * UNIT), cols], preferred_element_type=F32
                )
                part = both[: 2 * n] + both[2 * n :]
                if k == 4:
                    ACC[b][:, cols] = part[:n]
                    q[8, :, cols] = part[n:].astype(BF16)
                else:
                    to_left, to_right = part[:n], part[n:]
                    if k < 3 or first == 0:
                        to_right = to_right + q[k, :, cols].astype(F32)
                    if k < 3 or first > 0:
                        to_left = to_left + q[4 + k, :, cols].astype(F32)
                    q[k, :, cols] = to_right.astype(BF16)
                    q[4 + k, :, cols] = to_left.astype(BF16)

        for copy in sum_out(b, k):
            copy.start()

    def last_sum(b):
        for copy in sum_out(b, 1):
            copy.wait_recv()

    own0 = pltpu.make_async_copy(tb0, g0.at[3, pl.ds(0, 32)], own_sem.at[0])
    own1 = pltpu.make_async_copy(tb1, g1.at[3, pl.ds(0, 32)], own_sem.at[1])
    partner_in = remote(tbx, g1.at[3, pl.ds(32, 32)], xsend.at[0], xrecv.at[0], other_rep)
    own0.start()
    partner_in.start()
    own1.start()
    own0.wait()
    ring_start(0, 1)
    loads = [
        pltpu.make_async_copy(src, dst.at[0], load_sem.at[i])
        for i, (src, dst) in enumerate(((gate_hbm, wg), (up_hbm, wu), (down_hbm, wd)))
    ]
    pushes = [
        remote(src, dst.at[1], wsend.at[i], wrecv.at[i], other_core)
        for i, (src, dst) in enumerate(((gate_hbm, wg), (up_hbm, wu), (down_hbm, wd)))
    ]
    for copy in pushes + loads:
        copy.start()

    srow = lax.broadcasted_iota(jnp.int32, (META, 384), 0)
    scol = lax.broadcasted_iota(jnp.int32, (META, 384), 1)
    chosen = ((srow >> 5) == z) & (((srow >> 3) & 3) == (scol >> 7)) & ((srow & 7) == ((scol & 127) >> 4))
    sel[...] = jnp.where(chosen, 1.0, 0.0).astype(BF16)

    for k in range(1, 5):
        gather_step(0, k)
        if k == 4:
            own1.wait()
            partner_in.wait_recv()
            ring_start(1, 1)
        pack(0, k - 1)

    gather_step(1, 1)
    pack(1, 0)
    for copy in loads:
        copy.wait()
    for copy in pushes:
        copy.wait_recv()
    dispatch_wait(0, 0)
    dispatch_wait(0, 1)
    ffn(0, 0)
    gather_step(1, 2)
    pack(1, 1)
    gather_step(1, 3)
    pack(1, 2)
    dispatch_wait(0, 2)
    dispatch_wait(0, 3)
    ffn(0, 1)
    gather_step(1, 4)
    pack(1, 3)
    for j in (3, 2, 1, 0):
        give_back(0, j)
    dispatch_wait(1, 0)
    dispatch_wait(1, 1)
    ffn(1, 0)
    combine_step(0, 4)
    dispatch_wait(1, 2)
    dispatch_wait(1, 3)
    ffn(1, 1)
    for j in (3, 2, 1, 0):
        give_back(1, j)
    combine_step(0, 3)
    combine_step(0, 2)
    combine_step(0, 1)
    combine_step(1, 4)
    last_sum(0)
    out[0] = (acc0[...] + q0[0].astype(F32) + q0[4].astype(F32)).astype(BF16)
    combine_step(1, 3)
    combine_step(1, 2)
    combine_step(1, 1)
    last_sum(1)
    swap[0] = (acc1[32:, :] + q1[0, 32:].astype(F32) + q1[4, 32:].astype(F32)).astype(BF16)
    back = remote(swap.at[0], swap.at[1], xsend.at[1], xrecv.at[1], other_rep)
    back.start()
    acc1[:32, :] = acc1[:32, :] + q1[0, :32].astype(F32) + q1[4, :32].astype(F32)
    back.wait_recv()
    out[1] = (acc1[:32, :] + swap[1].astype(F32)).astype(BF16)

    back.wait_send()
    partner_in.wait_send()
    for copy in pushes:
        copy.wait_send()
    for b in range(2):
        for k in range(1, 5):
            for copy in ring_out(b, k) + sum_out(b, k):
                copy.wait_send()
        for j in range(PAIRS):
            for copy in dispatch_copies(b, j)[0] + return_copies(b, j)[0]:
                copy.wait_send()


def body(tokens, routing, route_gate, place_old, place_new, gate_proj, up_proj, down_proj):
    rep = lax.axis_index("rep")
    batches, rows, width = tokens.shape
    ff = gate_proj.shape[3]
    old_here = lax.dynamic_index_in_dim(place_old, rep, 0, keepdims=False)
    new_here = lax.dynamic_index_in_dim(place_new, rep, 0, keepdims=False)
    old_there = lax.dynamic_index_in_dim(place_old, 1 - rep, 0, keepdims=False)
    new_there = lax.dynamic_index_in_dim(place_new, 1 - rep, 0, keepdims=False)
    always = jnp.ones_like(old_here, dtype=bool)
    tb0 = token_block(tokens[0], routing[0], route_gate[0], old_here, always)
    tb1 = token_block(tokens[1], routing[1], route_gate[1], old_here, new_here == old_here)
    tbx = token_block(tokens[1], routing[1], route_gate[1], old_there, new_there != old_there)

    slots = PAIRS * PLANE * UNIT
    wide = width + META
    vm = pltpu.VMEM
    dma = pltpu.SemaphoreType.DMA
    anywhere = pl.BlockSpec(memory_space=pl.ANY)
    return pl.pallas_call(
        kernel,
        out_shape=jax.ShapeDtypeStruct((batches, rows, width), BF16),
        in_specs=[anywhere] * 6,
        out_specs=pl.BlockSpec(memory_space=pltpu.VMEM),
        scratch_shapes=[
            vm((2, width, ff), BF16),
            vm((2, width, ff), BF16),
            vm((2, ff, width), BF16),
            vm((PAIRS, 2 * rows, wide), BF16),
            vm((PAIRS, 4 * rows, wide), BF16),
            vm((slots, width), BF16),
            vm((slots, width), BF16),
            vm((slots, width), BF16),
            vm((slots, width), BF16),
            vm((slots, width), BF16),
            vm((slots, width), BF16),
            vm((9, rows, width), BF16),
            vm((9, 2 * rows, width), BF16),
            vm((PAIRS, 4 * rows, 128), BF16),
            vm((PAIRS, 8 * rows, 128), BF16),
            vm((rows, width), F32),
            vm((2 * rows, width), F32),
            vm((256, 2 * ff), BF16),
            vm((META, 384), BF16),
            vm((2, rows, width), BF16),
            dma((3,)),
            dma((3,)),
            dma((3,)),
            dma((2,)),
            dma((2,)),
            dma((2,)),
            dma((2, 4, 2)),
            dma((2, 4, 2)),
            dma((2, PAIRS, 7)),
            dma((2, PAIRS, 7)),
            dma((2, PAIRS)),
            dma((2, PAIRS, 7)),
            dma((2, PAIRS, 7)),
            dma((2, PAIRS)),
            dma((2, 4, 2)),
            dma((2, 4, 2)),
        ],
        compiler_params=pltpu.CompilerParams(
            collective_id=0, has_side_effects=True, vmem_limit_bytes=62 * MIB
        ),
        name="expert_layer",
    )(tb0, tb1, tbx, gate_proj[0, 0], up_proj[0, 0], down_proj[0, 0])


def solution(mesh):
    return jax.shard_map(
        body,
        mesh=mesh,
        in_specs=(
            P(None, ("rep", "ep"), None),
            P(None, ("rep", "ep"), None),
            P(None, ("rep", "ep"), None),
            P(),
            P(),
            P("rep", "ep", None, None),
            P("rep", "ep", None, None),
            P("rep", "ep", None, None),
        ),
        out_specs=P(None, ("rep", "ep"), None),
        check_vma=False,
    )
```

time: 389 us -> 211 us (0.54)
  waiting for transfers between devices: 264 us -> 0 us
  Pallas kernels: 0 us -> 199 us
  matrix products: 78.4 us -> 0.58 us
  starting transfers between devices: 37.4 us -> 0 us
    all_to_all x4 -> x0, waiting for transfers between devices: 238 us -> none  [a2a(): lax.all_to_all(x, 'ep', split_axis=0, concat_axis=0, axis_index_groups=gr...]
    pallas_call x0 -> x1, Pallas kernels: none -> 199 us  [body(): pl.pallas_call(kernel, out_shape=jax.ShapeDtypeStruct((batches, rows, wid...]
    dot_general x14 -> x3, matrix products: 78.4 us -> 0.58 us  [token_block(): rank = jnp.dot(before, named.astype(BF16), preferred_element_type=F32)]
    all_to_all x4 -> x0, starting transfers between devices: 31.2 us -> none  [a2a(): lax.all_to_all(x, 'ep', split_axis=0, concat_axis=0, axis_index_groups=gr...]
    ppermute x7 -> x0, waiting for transfers between devices: 26.6 us -> none  [the longest x1 6.68 us: body(): returned = lax.ppermute(outs[1][rows:].astype(BF16), 'rep', swap_rep)]
    ppermute x7 -> x0, starting transfers between devices: 6.17 us -> none  [the longest x1 2.82 us: body(): their_tokens = lax.ppermute(tokens[1], 'rep', swap_rep)]
  transfers between devices with their start and end apart: 11 -> 0, of which waited for: 9 -> 0; matrix products, arithmetic and copies ran while one was open for 19% -> 0% of each run, Pallas kernels for 0% -> 0%
where the time goes in v2:
time: 211 us; the launch traced here: 208 us
  Pallas kernels  199 us (94%)
  local copies, waits for them, and re-layouts  5.62 us (3%)
  other arithmetic  3.17 us (2%)
    pallas_call x1, Pallas kernels, body(): pl.pallas_call(kernel, out_shape=jax.ShapeDtypeStruct((batches, rows, wid...  199 us

profile of v2, /device:TPU:4, one launch (start us, length us, event | category | flops | bytes accessed | tf_op | source)
XLA Modules:
  0.0 208.3 jit_solution(17411678947888503288)
XLA Ops:
  0.0 0.1 pad.17.clone
  0.1 0.8 fusion.24
  0.8 0.7 slice_bitcast_fusion.5
  1.6 0.7 slice_bitcast_fusion.4
  2.3 0.1 copy.29
  2.3 0.1 copy.31
  2.4 0.1 copy.35
  2.5 0.2 fusion.4
  2.7 0.2 fusion.2
  2.9 0.1 copy.41
  3.0 0.2 fusion.1
  3.2 0.2 fusion
  3.4 0.1 copy.30
  3.5 0.1 copy.36
  3.6 0.1 copy.37
  3.7 0.2 select_reduce_fusion
  3.9 0.1 copy.42
  4.0 0.1 copy.38
  4.1 0.1 reduce-precision_convert_fusion
  4.1 0.1 copy.32
  4.2 0.3 maximum_bitcast_fusion.2
  4.6 0.1 copy.44
  4.7 0.1 copy.39
  4.8 0.1 copy.40
  4.8 0.1 copy.33
  4.9 0.1 copy.34
  5.0 1.1 slice_bitcast_fusion
  6.1 0.7 pad_maximum_fusion.tb0
  6.8 0.8 pad_maximum_fusion.2
  7.6 198.9 %expert_layer.1 = bf16[2,32,3584]{2,1,0:T(8,128)(2,1)} custom-call(bf16[32,3840]{1,0:T(8,128)(2,1)} %pad_maximum_fusion.tb0, bf16[32,3840]{1,0:T(8,128)(2,1)} %get-tuple-element.18.tb1, bf16[32,3840]{1,0:T(8,128)(2,1)} %get-tuple-element.17.tbx, bf16[3584,512]{1,0:T(8,128)(2,1)} %bitcast.48, bf16[3584,512]{1,0:T(8,128)(2,1)} %bitcast.49, ...), custom_call_target="tpu_custom_call" | custom-call | tf_op jit(solution)/shard_map/expert_layer/pallas_call | solution.py:341
  206.5 1.8 copy.46
  (3 shorter events, 0.1 us)

commit v3 on v2

v3 whole, which is shorter than its diff:
```python
import jax
import jax.numpy as jnp
from jax import lax
from jax.experimental import pallas as pl
from jax.experimental.pallas import tpu as pltpu
from jax.sharding import PartitionSpec as P

CAP = 8
BF16 = jnp.bfloat16
F32 = jnp.float32
NY, NZ, NX = 4, 8, 2
PLANE = NY * NX
PAIRS = 4
UNIT = 2 * CAP
META = 256
MESH = pl.DeviceIdType.MESH
MIB = 1 << 20


def kernel(
    tokens, routing, route_gate, places, gate_hbm, up_hbm, down_hbm, out,
    wg, wu, wd, g0, g1, s0, s1, r0, r1, t0, t1, q0, q1, w0, w1, acc0, acc1, hid, sel, swap, theirs,
    load_sem, wsend, wrecv, own_sem, xsend, xrecv,
    gsend, grecv, dsend, drecv, dloc, csend, crecv, cloc, rsend, rrecv,
):
    width = out.shape[2]
    wide = width + META
    half = width // 2
    tile = 512
    rows_of = (32, 64)
    block = PLANE * UNIT
    rep = lax.axis_index("rep")
    ep = lax.axis_index("ep")
    core = lax.rem(ep, 2)
    x = lax.rem(lax.div(ep, 2), NX)
    z = lax.rem(lax.div(ep, 2 * NX), NZ)
    y = lax.div(ep, 2 * NX * NZ)
    here = y * NX + x
    def at(yy, zz, xx):
        return (rep, ((yy * NZ + zz) * NX + xx) * 2 + core)

    right = at(y, lax.rem(z + 1, NZ), x)
    left = at(y, lax.rem(z + NZ - 1, NZ), x)
    other_rep = (1 - rep, ep)
    other_core = (rep, ep + 1 - 2 * core)
    plane = []
    for d in range(1, PLANE):
        yy, xx = lax.rem(y + d // NX, NY), lax.rem(x + d % NX, NX)
        plane.append((yy * NX + xx, at(yy, z, xx)))

    barrier = pltpu.get_barrier_semaphore()
    partners = [right, left, other_rep, other_core] + [dev for _, dev in plane]
    for dev in partners:
        pl.semaphore_signal(barrier, inc=1, device_id=dev, device_id_type=MESH)
    mine = pl.ds(0, 32)
    own = [
        pltpu.make_async_copy(tokens.at[b], g.at[3, mine, pl.ds(0, width)], own_sem.at[b])
        for b, g in enumerate((g0, g1))
    ]
    for copy in own:
        copy.start()

    first = rep == 0
    old_here = jnp.where(first, places[0:1, :], places[1:2, :])
    old_there = jnp.where(first, places[1:2, :], places[0:1, :])
    moved_here = old_here != jnp.where(first, places[2:3, :], places[3:4, :])
    moved_there = old_there != jnp.where(first, places[3:4, :], places[2:3, :])
    before = (
        lax.broadcasted_iota(jnp.int32, (32, 32), 0) > lax.broadcasted_iota(jnp.int32, (32, 32), 1)
    ).astype(F32)
    lower = lax.broadcasted_iota(jnp.int32, (32, 128), 1) < 64

    def describe(b, layout, served, ref):
        weight = jnp.zeros((32, 128), F32)
        named = jnp.zeros((32, 128), F32)
        for k in range(routing.shape[2]):
            hit = (routing[b, :, k : k + 1] == layout) & served
            weight = weight + jnp.where(hit, route_gate[b, :, k : k + 1], 0.0)
            named = named + jnp.where(hit, 1.0, 0.0)
        rank = jnp.dot(before.astype(BF16), named.astype(BF16), preferred_element_type=F32)
        rank = jnp.where(named > 0.5, rank, -1.0)
        high = weight.astype(BF16).astype(F32)
        ref[:, :128] = jnp.where(lower, rank, high).astype(BF16)
        ref[:, 128:] = jnp.where(lower, weight - high, 0.0).astype(BF16)

    lanes = pl.ds(width, META)
    describe(0, old_here, old_here >= 0, g0.at[3, mine, lanes])
    describe(1, old_here, ~moved_here, g1.at[3, mine, lanes])
    describe(1, old_there, moved_there, theirs)
    pl.semaphore_wait(barrier, len(partners))

    def remote(src, dst, send, recv, dev):
        return pltpu.make_async_remote_copy(
            src_ref=src, dst_ref=dst, send_sem=send, recv_sem=recv, device_id=dev, device_id_type=MESH
        )

    def unit(p, j, count=UNIT):
        return pl.ds(pl.multiple_of(j * block + p * UNIT, UNIT), count)

    G, S, R, T, Q, W, ACC = (g0, g1), (s0, s1), (r0, r1), (t0, t1), (q0, q1), (w0, w1), (acc0, acc1)

    def ways(k, c):
        return (0, 1) if k < 4 else (c,)

    def ring(b, k, way, c):
        g, n = G[b], rows_of[b]
        chunk = n // 2
        src = g.at[3, pl.ds(c * chunk, chunk)] if k == 1 else g.at[k - 2, pl.ds(way * n + c * chunk, chunk)]
        dst = g.at[k - 1, pl.ds((way if k < 4 else 1) * n + c * chunk, chunk)]
        sems = (gsend.at[b, k - 1, way, c], grecv.at[b, k - 1, way, c])
        return remote(src, dst, *sems, left if way else right)

    def ring_start(b, c):
        for way in ways(1, c):
            ring(b, 1, way, c).start()

    def gather_step(b, k):
        for c in range(2):
            for way in ways(k, c):
                ring(b, k, way, c).wait_recv()
                if k < 4 and way in ways(k + 1, c):
                    ring(b, k + 1, way, c).start()

    def dispatch_copies(b, j):
        remotes = [
            remote(S[b].at[unit(p, j)], R[b].at[unit(here, j)], dsend.at[b, j, d], drecv.at[b, j, d], dev)
            for d, (p, dev) in enumerate(plane)
        ]
        return remotes, pltpu.make_async_copy(S[b].at[unit(here, j)], R[b].at[unit(here, j)], dloc.at[b, j])

    def pack(b, j):
        g, s, w, n = G[b], S[b], W[b], rows_of[b]
        meta = jnp.dot(g[j, :, width:], sel[...], preferred_element_type=F32)
        lane = lax.broadcasted_iota(jnp.int32, (2 * n, 128), 1)
        row = lax.broadcasted_iota(jnp.int32, (2 * n, 128), 0)
        fits = (meta[:, :128] == (lane & 7).astype(F32)) & (((lane >> 3) & 1) == (row >= n).astype(jnp.int32))
        w[j, : 2 * n] = jnp.where(fits, meta[:, 128:256], 0.0).astype(BF16)
        w[j, 2 * n :] = jnp.where(fits, meta[:, 256:], 0.0).astype(BF16)
        pick = jnp.where(fits, 1.0, 0.0).T.astype(BF16)

        @pl.loop(0, width // tile)
        def _(i):
            cols = pl.ds(pl.multiple_of(i * tile, tile), tile)
            s[pl.ds(j * block, block), cols] = jnp.dot(
                pick, g[j, :, cols], preferred_element_type=F32
            ).astype(BF16)

        remotes, local = dispatch_copies(b, j)
        for copy in remotes:
            copy.start()
        local.start()

    def dispatch_wait(b, j):
        remotes, local = dispatch_copies(b, j)
        for copy in remotes:
            copy.wait_recv()
        local.wait()

    def ffn(b, m):
        rows = pl.ds(m * 256, 256)
        r = R[b]

        @pl.loop(0, 4)
        def _(i):
            h = lax.div(i, 2)
            cols = pl.ds(pl.multiple_of(lax.rem(i, 2) * 256, 256), 256)
            gate = jnp.dot(r[rows, :], wg[h, :, cols], preferred_element_type=F32)
            up = jnp.dot(r[rows, :], wu[h, :, cols], preferred_element_type=F32)
            hid[:, pl.ds(pl.multiple_of(i * 256, 256), 256)] = (jax.nn.silu(gate) * up).astype(BF16)

        @pl.loop(0, width // tile)
        def _(i):
            cols = pl.ds(pl.multiple_of(i * tile, tile), tile)
            down = jnp.dot(hid[:, :512], wd[0, :, cols], preferred_element_type=F32)
            down = down + jnp.dot(hid[:, 512:], wd[1, :, cols], preferred_element_type=F32)
            r[rows, cols] = down.astype(BF16)

    def return_copies(b, j):
        remotes = [
            remote(R[b].at[unit(p, j)], T[b].at[unit(here, j)], csend.at[b, j, d], crecv.at[b, j, d], dev)
            for d, (p, dev) in enumerate(plane)
        ]
        return remotes, [pltpu.make_async_copy(R[b].at[unit(here, j)], T[b].at[unit(here, j)], cloc.at[b, j])]

    def give_back(b, j):
        remotes, locals_ = return_copies(b, j)
        for copy in remotes + locals_:
            copy.start()

    def sums(b, k, h):
        q = Q[b]
        cols = pl.ds(h * half, half)
        copies = []
        for way in ways(k, h):
            src = q.at[8, :, cols] if k == 4 else q.at[4 * way + k, :, cols]
            dst = q.at[4 * way + k - 1, :, cols]
            sems = (rsend.at[b, k - 1, way, h], rrecv.at[b, k - 1, way, h])
            copies.append(remote(src, dst, *sems, left if way else right))
        return copies

    def combine_step(b, k, then=()):
        q, t, w, n = Q[b], T[b], W[b], rows_of[b]
        j = k - 1
        remotes, locals_ = return_copies(b, j)
        for copy in remotes:
            copy.wait_recv()
        for copy in locals_:
            copy.wait()
        for later in then:
            give_back(*later)
        for h in range(2):
            if k < 4:
                for copy in sums(b, k + 1, h):
                    copy.wait_recv()

            @pl.loop(0, half // 256)
            def _(i):
                cols = pl.ds(pl.multiple_of(h * half + i * 256, 256), 256)
                both = jnp.dot(w[j], t[pl.ds(j * block, block), cols], preferred_element_type=F32)
                part = both[: 2 * n] + both[2 * n :]
                if k == 4:
                    ACC[b][:, cols] = part[:n]
                    q[8, :, cols] = part[n:].astype(BF16)
                else:
                    to_left, to_right = part[:n], part[n:]
                    if k < 3 or h == 0:
                        to_right = to_right + q[k, :, cols].astype(F32)
                    if k < 3 or h == 1:
                        to_left = to_left + q[4 + k, :, cols].astype(F32)
                    q[k, :, cols] = to_right.astype(BF16)
                    q[4 + k, :, cols] = to_left.astype(BF16)

            for copy in sums(b, k, h):
                copy.start()

    def arrived(b):
        for h in range(2):
            for copy in sums(b, 1, h):
                copy.wait_recv()

    swap_in = [
        remote(tokens.at[1], g1.at[3, pl.ds(32, 32), pl.ds(0, width)], xsend.at[0], xrecv.at[0], other_rep),
        remote(theirs, g1.at[3, pl.ds(32, 32), lanes], xsend.at[1], xrecv.at[1], other_rep),
    ]
    swap_out = remote(swap.at[0], swap.at[1], xsend.at[2], xrecv.at[2], other_rep)
    for copy in own:
        copy.wait()
    ring_start(0, 0)
    ring_start(0, 1)
    for copy in swap_in:
        copy.start()
    loads = [
        pltpu.make_async_copy(src, dst.at[0], load_sem.at[i])
        for i, (src, dst) in enumerate(((gate_hbm, wg), (up_hbm, wu), (down_hbm, wd)))
    ]
    pushes = [
        remote(src, dst.at[1], wsend.at[i], wrecv.at[i], other_core)
        for i, (src, dst) in enumerate(((gate_hbm, wg), (up_hbm, wu), (down_hbm, wd)))
    ]
    for copy in pushes + loads:
        copy.start()

    lane_of = lax.broadcasted_iota(jnp.int32, (META, 384), 0)
    slot = lax.broadcasted_iota(jnp.int32, (META, 384), 1)
    place = lane_of & 63
    chosen = ((lane_of >> 6) == (slot >> 7)) & (((place >> 1) & (NZ - 1)) == z)
    chosen = chosen & (NX * (place >> 4) + (place & 1) == ((slot & 127) >> 4))
    sel[...] = jnp.where(chosen, 1.0, 0.0).astype(BF16)

    for k in range(1, 5):
        gather_step(0, k)
        if k == 3:
            for copy in swap_in:
                copy.wait_recv()
            ring_start(1, 0)
            ring_start(1, 1)
        pack(0, k - 1)

    gather_step(1, 1)
    pack(1, 0)
    for copy in loads:
        copy.wait()
    for copy in pushes:
        copy.wait_recv()
    dispatch_wait(0, 0)
    dispatch_wait(0, 1)
    ffn(0, 0)
    gather_step(1, 2)
    pack(1, 1)
    dispatch_wait(0, 2)
    dispatch_wait(0, 3)
    ffn(0, 1)
    gather_step(1, 3)
    pack(1, 2)
    gather_step(1, 4)
    pack(1, 3)
    dispatch_wait(1, 0)
    dispatch_wait(1, 1)
    give_back(0, 3)
    ffn(1, 0)
    dispatch_wait(1, 2)
    give_back(0, 2)
    dispatch_wait(1, 3)
    ffn(1, 1)
    give_back(1, 3)
    give_back(1, 2)
    combine_step(0, 4, [(1, 1)])
    combine_step(0, 3, [(1, 0)])
    combine_step(1, 4, [(0, 1)])
    combine_step(1, 3, [(0, 0)])
    combine_step(1, 2)
    combine_step(1, 1)
    combine_step(0, 2)
    arrived(1)
    swap[0] = (acc1[32:, :] + q1[0, 32:].astype(F32) + q1[4, 32:].astype(F32)).astype(BF16)
    swap_out.start()
    acc1[:32, :] = acc1[:32, :] + q1[0, :32].astype(F32) + q1[4, :32].astype(F32)
    combine_step(0, 1)
    swap_out.wait_recv()
    out[1] = (acc1[:32, :] + swap[1].astype(F32)).astype(BF16)
    arrived(0)
    out[0] = (acc0[...] + q0[0].astype(F32) + q0[4].astype(F32)).astype(BF16)

    for copy in pushes + swap_in + [swap_out]:
        copy.wait_send()
    for b in range(2):
        for k in range(1, 5):
            for c in range(2):
                for copy in [ring(b, k, way, c) for way in ways(k, c)] + sums(b, k, c):
                    copy.wait_send()
    for b in range(2):
        for j in range(PAIRS):
            for copy in dispatch_copies(b, j)[0] + return_copies(b, j)[0]:
                copy.wait_send()


def body(tokens, routing, route_gate, place_old, place_new, gate_proj, up_proj, down_proj):
    batches, rows, width = tokens.shape
    ff = gate_proj.shape[3]
    places = jnp.concatenate([place_old, place_new])
    places = jnp.concatenate([places, places], axis=1)

    slots = PAIRS * PLANE * UNIT
    wide = width + META
    vm = pltpu.VMEM
    dma = pltpu.SemaphoreType.DMA
    anywhere = pl.BlockSpec(memory_space=pl.ANY)
    local = pl.BlockSpec(memory_space=pltpu.VMEM)
    return pl.pallas_call(
        kernel,
        out_shape=jax.ShapeDtypeStruct((batches, rows, width), BF16),
        in_specs=[anywhere, local, local, local, anywhere, anywhere, anywhere],
        out_specs=local,
        scratch_shapes=[
            vm((2, width, ff), BF16),
            vm((2, width, ff), BF16),
            vm((2, ff, width), BF16),
            vm((PAIRS, 2 * rows, wide), BF16),
            vm((PAIRS, 4 * rows, wide), BF16),
            vm((slots, width), BF16),
            vm((slots, width), BF16),
            vm((slots, width), BF16),
            vm((slots, width), BF16),
            vm((slots, width), BF16),
            vm((slots, width), BF16),
            vm((9, rows, width), BF16),
            vm((9, 2 * rows, width), BF16),
            vm((PAIRS, 4 * rows, 128), BF16),
            vm((PAIRS, 8 * rows, 128), BF16),
            vm((rows, width), F32),
            vm((2 * rows, width), F32),
            vm((256, 2 * ff), BF16),
            vm((META, 384), BF16),
            vm((2, rows, width), BF16),
            vm((rows, META), BF16),
            dma((3,)),
            dma((3,)),
            dma((3,)),
            dma((2,)),
            dma((3,)),
            dma((3,)),
            dma((2, 4, 2, 2)),
            dma((2, 4, 2, 2)),
            dma((2, PAIRS, 7)),
            dma((2, PAIRS, 7)),
            dma((2, PAIRS)),
            dma((2, PAIRS, 7)),
            dma((2, PAIRS, 7)),
            dma((2, PAIRS)),
            dma((2, 4, 2, 2)),
            dma((2, 4, 2, 2)),
        ],
        compiler_params=pltpu.CompilerParams(
            collective_id=0, has_side_effects=True, vmem_limit_bytes=62 * MIB
        ),
        name="expert_layer",
    )(tokens, routing, route_gate, places, gate_proj[0, 0], up_proj[0, 0], down_proj[0, 0])


def solution(mesh):
    return jax.shard_map(
        body,
        mesh=mesh,
        in_specs=(
            P(None, ("rep", "ep"), None),
            P(None, ("rep", "ep"), None),
            P(None, ("rep", "ep"), None),
            P(),
            P(),
            P("rep", "ep", None, None),
            P("rep", "ep", None, None),
            P("rep", "ep", None, None),
        ),
        out_specs=P(None, ("rep", "ep"), None),
        check_vma=False,
    )
```

time: 211 us -> 196 us (0.929)
  Pallas kernels: 199 us -> 189 us
    pallas_call x1, Pallas kernels: 199 us -> 189 us  [body(): pl.pallas_call(kernel, out_shape=jax.ShapeDtypeStruct((batches, rows, wid...]
    unnamed x1 -> x3, local copies, waits for them, and re-layouts: 1.82 us -> 4.59 us
where the time goes in v3:
time: 196 us; the launch traced here: 195 us
  Pallas kernels  189 us (96%)
  local copies, waits for them, and re-layouts  4.59 us (2%)
    pallas_call x1, Pallas kernels, body(): pl.pallas_call(kernel, out_shape=jax.ShapeDtypeStruct((batches, rows, wid...  189 us
    unnamed x3, local copies, waits for them, and re-layouts  4.59 us

profile of v3, /device:TPU:4, one launch (start us, length us, event | category | flops | bytes accessed | tf_op | source)
XLA Modules:
  0.0 195.4 jit_solution(2159780447717801991)
XLA Ops:
  0.0 1.4 add_add_fusion.places
  1.4 1.4 copy.9.routing
  2.8 1.4 copy.10.route_gate
  4.2 189.4 %expert_layer.1 = bf16[2,32,3584]{2,1,0:T(8,128)(2,1)} custom-call(bf16[2,32,3584]{2,1,0:T(8,128)(2,1)} %tokens.1, s32[2,32,8]{2,1,0:T(8,128)} %copy.9.routing, f32[2,32,8]{2,1,0:T(8,128)} %copy.10.route_gate, s32[4,128]{1,0:T(4,128)} %add_add_fusion.places, bf16[3584,512]{1,0:T(8,128)(2,1)} %bitcast.3, bf16[3584,512]{1,0:T(8,128)(2,1)} %bitcast.4, ...), custom_call_target="tpu_custom_call" | custom-call | tf_op jit(solution)/shard_map/expert_layer/pallas_call | solution.py:349
  193.6 1.8 copy.12

commit v4 on v3

--- a/solution.py
+++ b/solution.py
@@ -18,7 +18,7 @@
 
 
 def kernel(
-    tokens, routing, route_gate, places, gate_hbm, up_hbm, down_hbm, out,
+    tokens, routing, route_gate, place_old, place_new, gate_hbm, up_hbm, down_hbm, out,
     wg, wu, wd, g0, g1, s0, s1, r0, r1, t0, t1, q0, q1, w0, w1, acc0, acc1, hid, sel, swap, theirs,
     load_sem, wsend, wrecv, own_sem, xsend, xrecv,
     gsend, grecv, dsend, drecv, dloc, csend, crecv, cloc, rsend, rrecv,
@@ -61,21 +61,24 @@
         copy.start()
 
     first = rep == 0
-    old_here = jnp.where(first, places[0:1, :], places[1:2, :])
-    old_there = jnp.where(first, places[1:2, :], places[0:1, :])
-    moved_here = old_here != jnp.where(first, places[2:3, :], places[3:4, :])
-    moved_there = old_there != jnp.where(first, places[3:4, :], places[2:3, :])
+    old = jnp.concatenate([place_old[...], place_old[...]], axis=1)
+    new = jnp.concatenate([place_new[...], place_new[...]], axis=1)
+    old_here = jnp.where(first, old[0:1], old[1:2])
+    old_there = jnp.where(first, old[1:2], old[0:1])
+    moved_here = old_here != jnp.where(first, new[0:1], new[1:2])
+    moved_there = old_there != jnp.where(first, new[1:2], new[0:1])
     before = (
         lax.broadcasted_iota(jnp.int32, (32, 32), 0) > lax.broadcasted_iota(jnp.int32, (32, 32), 1)
     ).astype(F32)
     lower = lax.broadcasted_iota(jnp.int32, (32, 128), 1) < 64
 
     def describe(b, layout, served, ref):
+        chosen, gates = routing[b].T, route_gate[b].T
         weight = jnp.zeros((32, 128), F32)
         named = jnp.zeros((32, 128), F32)
-        for k in range(routing.shape[2]):
-            hit = (routing[b, :, k : k + 1] == layout) & served
-            weight = weight + jnp.where(hit, route_gate[b, :, k : k + 1], 0.0)
+        for k in range(routing.shape[1]):
+            hit = (chosen[:, k : k + 1] == layout) & served
+            weight = weight + jnp.where(hit, gates[:, k : k + 1], 0.0)
             named = named + jnp.where(hit, 1.0, 0.0)
         rank = jnp.dot(before.astype(BF16), named.astype(BF16), preferred_element_type=F32)
         rank = jnp.where(named > 0.5, rank, -1.0)
@@ -269,7 +272,7 @@
 
     for k in range(1, 5):
         gather_step(0, k)
-        if k == 3:
+        if k == 2:
             for copy in swap_in:
                 copy.wait_recv()
             ring_start(1, 0)
@@ -287,13 +290,13 @@
     ffn(0, 0)
     gather_step(1, 2)
     pack(1, 1)
-    dispatch_wait(0, 2)
-    dispatch_wait(0, 3)
-    ffn(0, 1)
     gather_step(1, 3)
     pack(1, 2)
     gather_step(1, 4)
     pack(1, 3)
+    dispatch_wait(0, 2)
+    dispatch_wait(0, 3)
+    ffn(0, 1)
     dispatch_wait(1, 0)
     dispatch_wait(1, 1)
     give_back(0, 3)
@@ -337,8 +340,6 @@
 def body(tokens, routing, route_gate, place_old, place_new, gate_proj, up_proj, down_proj):
     batches, rows, width = tokens.shape
     ff = gate_proj.shape[3]
-    places = jnp.concatenate([place_old, place_new])
-    places = jnp.concatenate([places, places], axis=1)
 
     slots = PAIRS * PLANE * UNIT
     wide = width + META
@@ -349,7 +350,7 @@
     return pl.pallas_call(
         kernel,
         out_shape=jax.ShapeDtypeStruct((batches, rows, width), BF16),
-        in_specs=[anywhere, local, local, local, anywhere, anywhere, anywhere],
+        in_specs=[anywhere] + [local] * 4 + [anywhere] * 3,
         out_specs=local,
         scratch_shapes=[
             vm((2, width, ff), BF16),
@@ -394,7 +395,16 @@
             collective_id=0, has_side_effects=True, vmem_limit_bytes=62 * MIB
         ),
         name="expert_layer",
-    )(tokens, routing, route_gate, places, gate_proj[0, 0], up_proj[0, 0], down_proj[0, 0])
+    )(
+        tokens,
+        jnp.swapaxes(routing, 1, 2),
+        jnp.swapaxes(route_gate, 1, 2),
+        place_old,
+        place_new,
+        gate_proj[0, 0],
+        up_proj[0, 0],
+        down_proj[0, 0],
+    )
 
 
 def solution(mesh):

time: 196 us -> 191 us (0.974)
  local copies, waits for them, and re-layouts: 4.59 us -> 1.82 us
    unnamed x3 -> x1, local copies, waits for them, and re-layouts: 4.59 us -> 1.82 us
where the time goes in v4:
time: 191 us
  Pallas kernels  189 us (99%)
    pallas_call x1, Pallas kernels, body(): pl.pallas_call(kernel, out_shape=jax.ShapeDtypeStruct((batches, rows, wid...  189 us

profile of v4, /device:TPU:4, one launch (start us, length us, event | category | flops | bytes accessed | tf_op | source)
XLA Modules:
  0.0 191.1 jit_solution(3139533608541159011)
XLA Ops:
  0.0 189.3 %expert_layer.1 = bf16[2,32,3584]{2,1,0:T(8,128)(2,1)} custom-call(bf16[2,32,3584]{2,1,0:T(8,128)(2,1)} %tokens.1, s32[2,8,32]{2,1,0:T(8,128)} %bitcast.8, f32[2,8,32]{2,1,0:T(8,128)} %bitcast.9, s32[2,64]{1,0:T(2,128)} %place_old.1, s32[2,64]{1,0:T(2,128)} %place_new.1, bf16[3584,512]{1,0:T(8,128)(2,1)} %bitcast.5, bf16[3584,512]{1,0:T(8,128)(2,1)} %bitcast.6, ...), custom_call_target="tpu_custom_call" | custom-call | tf_op jit(solution)/shard_map/expert_layer/pallas_call | solution.py:350
  189.3 1.8 copy.10

commit v5 on v4

--- a/solution.py
+++ b/solution.py
@@ -54,7 +54,7 @@
         pl.semaphore_signal(barrier, inc=1, device_id=dev, device_id_type=MESH)
     mine = pl.ds(0, 32)
     own = [
-        pltpu.make_async_copy(tokens.at[b], g.at[3, mine, pl.ds(0, width)], own_sem.at[b])
+        pltpu.make_async_copy(tokens.at[b], g.at[3, mine, pl.ds(META, width)], own_sem.at[b])
         for b, g in enumerate((g0, g1))
     ]
     for copy in own:
@@ -86,7 +86,7 @@
         ref[:, :128] = jnp.where(lower, rank, high).astype(BF16)
         ref[:, 128:] = jnp.where(lower, weight - high, 0.0).astype(BF16)
 
-    lanes = pl.ds(width, META)
+    lanes = pl.ds(0, META)
     describe(0, old_here, old_here >= 0, g0.at[3, mine, lanes])
     describe(1, old_here, ~moved_here, g1.at[3, mine, lanes])
     describe(1, old_there, moved_there, theirs)
@@ -107,9 +107,9 @@
 
     def ring(b, k, way, c):
         g, n = G[b], rows_of[b]
-        chunk = n // 2
-        src = g.at[3, pl.ds(c * chunk, chunk)] if k == 1 else g.at[k - 2, pl.ds(way * n + c * chunk, chunk)]
-        dst = g.at[k - 1, pl.ds((way if k < 4 else 1) * n + c * chunk, chunk)]
+        cols = pl.ds(META + half, half) if c else pl.ds(0, META + half)
+        src = g.at[3, pl.ds(0, n), cols] if k == 1 else g.at[k - 2, pl.ds(way * n, n), cols]
+        dst = g.at[k - 1, pl.ds((way if k < 4 else 1) * n, n), cols]
         sems = (gsend.at[b, k - 1, way, c], grecv.at[b, k - 1, way, c])
         return remote(src, dst, *sems, left if way else right)
 
@@ -117,47 +117,70 @@
         for way in ways(1, c):
             ring(b, 1, way, c).start()
 
+    def gather_chunk(b, k, c):
+        for way in ways(k, c):
+            ring(b, k, way, c).wait_recv()
+            if k < 4 and way in ways(k + 1, c):
+                ring(b, k + 1, way, c).start()
+
     def gather_step(b, k):
-        for c in range(2):
-            for way in ways(k, c):
-                ring(b, k, way, c).wait_recv()
-                if k < 4 and way in ways(k + 1, c):
-                    ring(b, k + 1, way, c).start()
-
-    def dispatch_copies(b, j):
+        gather_chunk(b, k, 0)
+        gather_chunk(b, k, 1)
+
+    def parts(b, j):
+        return 2 if (b, j) == (0, 0) else 1
+
+    def exchange(src, dst, sems, b, j, part):
+        send, recv, loc = sems
+        cols = pl.ds(part * half, half) if parts(b, j) == 2 else pl.ds(0, width)
+        to = dst.at[unit(here, j), cols]
         remotes = [
-            remote(S[b].at[unit(p, j)], R[b].at[unit(here, j)], dsend.at[b, j, d], drecv.at[b, j, d], dev)
+            remote(src.at[unit(p, j), cols], to, send.at[b, j, 7 * part + d], recv.at[b, j, 7 * part + d], dev)
             for d, (p, dev) in enumerate(plane)
         ]
-        return remotes, pltpu.make_async_copy(S[b].at[unit(here, j)], R[b].at[unit(here, j)], dloc.at[b, j])
-
-    def pack(b, j):
-        g, s, w, n = G[b], S[b], W[b], rows_of[b]
-        meta = jnp.dot(g[j, :, width:], sel[...], preferred_element_type=F32)
+        return remotes, pltpu.make_async_copy(src.at[unit(here, j), cols], to, loc.at[b, j, part])
+
+    def dispatch_copies(b, j, part):
+        return exchange(S[b], R[b], (dsend, drecv, dloc), b, j, part)
+
+    def begin(copies):
+        remotes, local = copies
+        for copy in remotes:
+            copy.start()
+        local.start()
+
+    def landed(copies):
+        remotes, local = copies
+        for copy in remotes:
+            copy.wait_recv()
+        local.wait()
+
+    def choose(b, j):
+        g, w, n = G[b], W[b], rows_of[b]
+        meta = jnp.dot(g[j, :, :META], sel[...], preferred_element_type=F32)
         lane = lax.broadcasted_iota(jnp.int32, (2 * n, 128), 1)
         row = lax.broadcasted_iota(jnp.int32, (2 * n, 128), 0)
         fits = (meta[:, :128] == (lane & 7).astype(F32)) & (((lane >> 3) & 1) == (row >= n).astype(jnp.int32))
         w[j, : 2 * n] = jnp.where(fits, meta[:, 128:256], 0.0).astype(BF16)
         w[j, 2 * n :] = jnp.where(fits, meta[:, 256:], 0.0).astype(BF16)
-        pick = jnp.where(fits, 1.0, 0.0).T.astype(BF16)
+        return jnp.where(fits, 1.0, 0.0).T.astype(BF16)
+
+    def pack(b, j, part, pick):
+        g, s = G[b], S[b]
+        step = tile // parts(b, j)
 
         @pl.loop(0, width // tile)
         def _(i):
-            cols = pl.ds(pl.multiple_of(i * tile, tile), tile)
-            s[pl.ds(j * block, block), cols] = jnp.dot(
-                pick, g[j, :, cols], preferred_element_type=F32
+            at_col = part * half + i * step
+            s[pl.ds(j * block, block), pl.ds(pl.multiple_of(at_col, 256), step)] = jnp.dot(
+                pick, g[j, :, pl.ds(pl.multiple_of(META + at_col, 256), step)], preferred_element_type=F32
             ).astype(BF16)
 
-        remotes, local = dispatch_copies(b, j)
-        for copy in remotes:
-            copy.start()
-        local.start()
+        begin(dispatch_copies(b, j, part))
 
     def dispatch_wait(b, j):
-        remotes, local = dispatch_copies(b, j)
-        for copy in remotes:
-            copy.wait_recv()
-        local.wait()
+        for part in range(parts(b, j)):
+            landed(dispatch_copies(b, j, part))
 
     def ffn(b, m):
         rows = pl.ds(m * 256, 256)
@@ -178,17 +201,12 @@
             down = down + jnp.dot(hid[:, 512:], wd[1, :, cols], preferred_element_type=F32)
             r[rows, cols] = down.astype(BF16)
 
-    def return_copies(b, j):
-        remotes = [
-            remote(R[b].at[unit(p, j)], T[b].at[unit(here, j)], csend.at[b, j, d], crecv.at[b, j, d], dev)
-            for d, (p, dev) in enumerate(plane)
-        ]
-        return remotes, [pltpu.make_async_copy(R[b].at[unit(here, j)], T[b].at[unit(here, j)], cloc.at[b, j])]
+    def return_copies(b, j, part):
+        return exchange(R[b], T[b], (csend, crecv, cloc), b, j, part)
 
     def give_back(b, j):
-        remotes, locals_ = return_copies(b, j)
-        for copy in remotes + locals_:
-            copy.start()
+        for part in range(parts(b, j)):
+            begin(return_copies(b, j, part))
 
     def sums(b, k, h):
         q = Q[b]
@@ -204,14 +222,12 @@
     def combine_step(b, k, then=()):
         q, t, w, n = Q[b], T[b], W[b], rows_of[b]
         j = k - 1
-        remotes, locals_ = return_copies(b, j)
-        for copy in remotes:
-            copy.wait_recv()
-        for copy in locals_:
-            copy.wait()
+        landed(return_copies(b, j, 0))
         for later in then:
             give_back(*later)
         for h in range(2):
+            if h and parts(b, j) == 2:
+                landed(return_copies(b, j, 1))
             if k < 4:
                 for copy in sums(b, k + 1, h):
                     copy.wait_recv()
@@ -236,13 +252,8 @@
             for copy in sums(b, k, h):
                 copy.start()
 
-    def arrived(b):
-        for h in range(2):
-            for copy in sums(b, 1, h):
-                copy.wait_recv()
-
     swap_in = [
-        remote(tokens.at[1], g1.at[3, pl.ds(32, 32), pl.ds(0, width)], xsend.at[0], xrecv.at[0], other_rep),
+        remote(tokens.at[1], g1.at[3, pl.ds(32, 32), pl.ds(META, width)], xsend.at[0], xrecv.at[0], other_rep),
         remote(theirs, g1.at[3, pl.ds(32, 32), lanes], xsend.at[1], xrecv.at[1], other_rep),
     ]
     swap_out = remote(swap.at[0], swap.at[1], xsend.at[2], xrecv.at[2], other_rep)
@@ -270,17 +281,22 @@
     chosen = chosen & (NX * (place >> 4) + (place & 1) == ((slot & 127) >> 4))
     sel[...] = jnp.where(chosen, 1.0, 0.0).astype(BF16)
 
-    for k in range(1, 5):
+    gather_chunk(0, 1, 0)
+    pick = choose(0, 0)
+    pack(0, 0, 0, pick)
+    gather_chunk(0, 1, 1)
+    pack(0, 0, 1, pick)
+    for k in range(2, 5):
         gather_step(0, k)
         if k == 2:
             for copy in swap_in:
                 copy.wait_recv()
             ring_start(1, 0)
             ring_start(1, 1)
-        pack(0, k - 1)
+        pack(0, k - 1, 0, choose(0, k - 1))
 
     gather_step(1, 1)
-    pack(1, 0)
+    pack(1, 0, 0, choose(1, 0))
     for copy in loads:
         copy.wait()
     for copy in pushes:
@@ -289,11 +305,11 @@
     dispatch_wait(0, 1)
     ffn(0, 0)
     gather_step(1, 2)
-    pack(1, 1)
+    pack(1, 1, 0, choose(1, 1))
     gather_step(1, 3)
-    pack(1, 2)
+    pack(1, 2, 0, choose(1, 2))
     gather_step(1, 4)
-    pack(1, 3)
+    pack(1, 3, 0, choose(1, 3))
     dispatch_wait(0, 2)
     dispatch_wait(0, 3)
     ffn(0, 1)
@@ -314,15 +330,20 @@
     combine_step(1, 2)
     combine_step(1, 1)
     combine_step(0, 2)
-    arrived(1)
+    for h in range(2):
+        for copy in sums(1, 1, h):
+            copy.wait_recv()
     swap[0] = (acc1[32:, :] + q1[0, 32:].astype(F32) + q1[4, 32:].astype(F32)).astype(BF16)
     swap_out.start()
     acc1[:32, :] = acc1[:32, :] + q1[0, :32].astype(F32) + q1[4, :32].astype(F32)
     combine_step(0, 1)
     swap_out.wait_recv()
     out[1] = (acc1[:32, :] + swap[1].astype(F32)).astype(BF16)
-    arrived(0)
-    out[0] = (acc0[...] + q0[0].astype(F32) + q0[4].astype(F32)).astype(BF16)
+    for h in range(2):
+        cols = pl.ds(h * half, half)
+        for copy in sums(0, 1, h):
+            copy.wait_recv()
+        out[0, :, cols] = (acc0[:, cols] + q0[0, :, cols].astype(F32) + q0[4, :, cols].astype(F32)).astype(BF16)
 
     for copy in pushes + swap_in + [swap_out]:
         copy.wait_send()
@@ -333,8 +354,9 @@
                     copy.wait_send()
     for b in range(2):
         for j in range(PAIRS):
-            for copy in dispatch_copies(b, j)[0] + return_copies(b, j)[0]:
-                copy.wait_send()
+            for part in range(parts(b, j)):
+                for copy in dispatch_copies(b, j, part)[0] + return_copies(b, j, part)[0]:
+                    copy.wait_send()
 
 
 def body(tokens, routing, route_gate, place_old, place_new, gate_proj, up_proj, down_proj):
@@ -382,12 +404,12 @@
             dma((3,)),
             dma((2, 4, 2, 2)),
             dma((2, 4, 2, 2)),
-            dma((2, PAIRS, 7)),
-            dma((2, PAIRS, 7)),
-            dma((2, PAIRS)),
-            dma((2, PAIRS, 7)),
-            dma((2, PAIRS, 7)),
-            dma((2, PAIRS)),
+            dma((2, PAIRS, 14)),
+            dma((2, PAIRS, 14)),
+            dma((2, PAIRS, 2)),
+            dma((2, PAIRS, 14)),
+            dma((2, PAIRS, 14)),
+            dma((2, PAIRS, 2)),
             dma((2, 4, 2, 2)),
             dma((2, 4, 2, 2)),
         ],

time: 191 us -> 190 us (level)
  no operation moved by 1% of the time
where the time goes in v5:
time: 190 us
  Pallas kernels  188 us (99%)
    pallas_call x1, Pallas kernels, body(): pl.pallas_call(kernel, out_shape=jax.ShapeDtypeStruct((batches, rows, wid...  188 us

profile of v5, /device:TPU:4, one launch (start us, length us, event | category | flops | bytes accessed | tf_op | source)
XLA Modules:
  0.0 189.6 jit_solution(4222257965989915784)
XLA Ops:
  0.0 187.7 %expert_layer.1 = bf16[2,32,3584]{2,1,0:T(8,128)(2,1)} custom-call(bf16[2,32,3584]{2,1,0:T(8,128)(2,1)} %tokens.1, s32[2,8,32]{2,1,0:T(8,128)} %bitcast.8, f32[2,8,32]{2,1,0:T(8,128)} %bitcast.9, s32[2,64]{1,0:T(2,128)} %place_old.1, s32[2,64]{1,0:T(2,128)} %place_new.1, bf16[3584,512]{1,0:T(8,128)(2,1)} %bitcast.5, bf16[3584,512]{1,0:T(8,128)(2,1)} %bitcast.6, ...), custom_call_target="tpu_custom_call" | custom-call | tf_op jit(solution)/shard_map/expert_layer/pallas_call | solution.py:372
  187.8 1.8 copy.10

commit v6 on v5

--- a/solution.py
+++ b/solution.py
@@ -44,7 +44,7 @@
     other_rep = (1 - rep, ep)
     other_core = (rep, ep + 1 - 2 * core)
     plane = []
-    for d in range(1, PLANE):
+    for d in (1, 2, 6, 3, 7, 4, 5):
         yy, xx = lax.rem(y + d // NX, NY), lax.rem(x + d % NX, NX)
         plane.append((yy * NX + xx, at(yy, z, xx)))
 
@@ -57,7 +57,11 @@
         pltpu.make_async_copy(tokens.at[b], g.at[3, mine, pl.ds(META, width)], own_sem.at[b])
         for b, g in enumerate((g0, g1))
     ]
-    for copy in own:
+    loads = [
+        pltpu.make_async_copy(src, dst.at[0], load_sem.at[i])
+        for i, (src, dst) in enumerate(((gate_hbm, wg), (up_hbm, wu), (down_hbm, wd)))
+    ]
+    for copy in own + loads:
         copy.start()
 
     first = rep == 0
@@ -263,15 +267,11 @@
     ring_start(0, 1)
     for copy in swap_in:
         copy.start()
-    loads = [
-        pltpu.make_async_copy(src, dst.at[0], load_sem.at[i])
-        for i, (src, dst) in enumerate(((gate_hbm, wg), (up_hbm, wu), (down_hbm, wd)))
-    ]
     pushes = [
         remote(src, dst.at[1], wsend.at[i], wrecv.at[i], other_core)
         for i, (src, dst) in enumerate(((gate_hbm, wg), (up_hbm, wu), (down_hbm, wd)))
     ]
-    for copy in pushes + loads:
+    for copy in pushes:
         copy.start()
 
     lane_of = lax.broadcasted_iota(jnp.int32, (META, 384), 0)

time: 190 us -> 192 us (1.011)
  no operation moved by 1% of the time
where the time goes in v6:
time: 192 us; the launch traced here: 191 us
  Pallas kernels  189 us (98%)
    pallas_call x1, Pallas kernels, body(): pl.pallas_call(kernel, out_shape=jax.ShapeDtypeStruct((batches, rows, wid...  189 us

profile of v6, /device:TPU:4, one launch (start us, length us, event | category | flops | bytes accessed | tf_op | source)
XLA Modules:
  0.0 191.3 jit_solution(11026305052710352775)
XLA Ops:
  0.0 189.5 %expert_layer.1 = bf16[2,32,3584]{2,1,0:T(8,128)(2,1)} custom-call(bf16[2,32,3584]{2,1,0:T(8,128)(2,1)} %tokens.1, s32[2,8,32]{2,1,0:T(8,128)} %bitcast.8, f32[2,8,32]{2,1,0:T(8,128)} %bitcast.9, s32[2,64]{1,0:T(2,128)} %place_old.1, s32[2,64]{1,0:T(2,128)} %place_new.1, bf16[3584,512]{1,0:T(8,128)(2,1)} %bitcast.5, bf16[3584,512]{1,0:T(8,128)(2,1)} %bitcast.6, ...), custom_call_target="tpu_custom_call" | custom-call | tf_op jit(solution)/shard_map/expert_layer/pallas_call | solution.py:372
  189.5 1.8 copy.10
